TPU v7x, 32 devices: a whole 2x2x4 slice. The times are simulated.
32 devices in a mesh: grp: 8 (over z, y), head: 4 (over x, core).
Axes of the slice: x: 2, y: 2, z: 4, core: 2. Of those that a mesh axis runs over, the one named last changes fastest.
Arguments:
- activations: bfloat16 [256, 4096], P('grp', 'head'), may hold values from -1.5 to 1.5
- ln_gain: bfloat16 [4096], replicated, may hold values from 0.099609375 to 1.8984375
- ln_bias: bfloat16 [4096], replicated, may hold values from -3 to 3
- w_qkv: bfloat16 [4096, 3, 4096], P('grp', None, 'head'), may hold values from -0.09375 to 0.09375
- prefix_keys: bfloat16 [16, 1024, 4096], P('grp', None, 'head')
- prefix_values: bfloat16 [16, 1024, 4096], P('grp', None, 'head'), may hold values from -6 to 6
- own_keys: bfloat16 [256, 32, 4096], P('grp', None, 'head'), may hold values from -6 to 6
- own_values: bfloat16 [256, 32, 4096], P('grp', None, 'head'), may hold values from -6 to 6
- prompt_len: int32 [16], P('grp'), may hold values from 64 to 1024, as said below
- own_len: int32 [256], P('grp'), may hold values from 1 to 32, as said below
- w_attn_out: bfloat16 [256, 16, 4096], P('grp', 'head'), may hold values from -0.09375 to 0.09375
- w_in: bfloat16 [4096, 16384], P(None, ('grp', 'head')), may hold values from -0.09375 to 0.09375
- b_in: bfloat16 [16384], P(('grp', 'head')), may hold values from -4 to 4
- w_down: bfloat16 [16384, 4096], P(('grp', 'head')), may hold values from -0.046875 to 0.046875
- b_down: bfloat16 [4096], P('head'), may hold values from -3 to 3
Outputs:
- layer_out: bfloat16 [256, 4096], P('grp', 'head')
Inputs may be any that keep to these rules, and one draw needn't show every extreme that they name: `prompt_len`: some group's prompt has exactly 1024 tokens and some has 64. `own_len`: some request has exactly 32 own tokens.
All inputs are finite; a program needn't handle non-finite values.
Results may differ from a plain program's by a relative error of at most 0.034.
Values may be sent and summed in bfloat16 or wider, within the bound.
A program may use at most 128 MiB of HBM per device.

v0:
```python
import math

import jax
import jax.numpy as jnp
from jax import lax
from jax.sharding import PartitionSpec as P

HS = 256
ROT = 64
GSIZE = 16


def normalize(rows, gain, shift):
    floats = rows.astype(jnp.float32)
    center = floats - jnp.mean(floats, axis=-1, keepdims=True)
    spread = jnp.mean(center * center, axis=-1, keepdims=True)
    return (
        center * lax.rsqrt(spread + 1e-05) * gain.astype(jnp.float32) + shift.astype(jnp.float32)
    ).astype(jnp.bfloat16)


def rotate(values, positions):
    half = ROT // 2
    index = jnp.arange(half, dtype=jnp.float32)
    freqs = jnp.power(jnp.float32(10000.0), -2.0 * index / ROT)
    angle = positions[:, None, None] * freqs[None, None, :]
    cosine = jnp.cos(angle)
    sine = jnp.sin(angle)
    pairs = values[..., :ROT].reshape(values.shape[:-1] + (half, 2))
    first = pairs[..., 0]
    second = pairs[..., 1]
    turned = jnp.stack([first * cosine - second * sine, second * cosine + first * sine], axis=-1)
    turned = turned.reshape(values.shape[:-1] + (ROT,))
    return jnp.concatenate([turned, values[..., ROT:]], axis=-1)


def local(
    activations,
    ln_gain,
    ln_bias,
    w_qkv,
    prefix_keys,
    prefix_values,
    own_keys,
    own_values,
    prompt_len,
    own_len,
    w_attn_out,
    w_in,
    b_in,
    w_down,
    b_down,
):
    grp_count = lax.axis_size("grp")
    head_count = lax.axis_size("head")
    width_here = activations.shape[1]
    full_rows = lax.all_gather(activations, "head", axis=1, tiled=True)
    normed = normalize(full_rows, ln_gain, ln_bias)
    local_rows = normed.shape[0]
    groups_here = prompt_len.shape[0]
    columns = lax.all_to_all(normed, "grp", split_axis=1, concat_axis=0, tiled=True)
    qkv = lax.psum_scatter(
        jnp.einsum("rf,fch->rch", columns, w_qkv, preferred_element_type=jnp.float32).astype(
            jnp.bfloat16
        ),
        "grp",
        scatter_dimension=0,
        tiled=True,
    ).astype(jnp.float32)
    heads_here = w_qkv.shape[2] // HS
    member = (jnp.arange(local_rows) // GSIZE)[:, None] == jnp.arange(groups_here)[None, :]
    row_prompt = jnp.sum(jnp.where(member, prompt_len[None, :], 0), axis=1)
    positions = (row_prompt + own_len).astype(jnp.float32)
    query = rotate(qkv[:, 0].reshape(local_rows, heads_here, HS), positions).astype(jnp.bfloat16)
    key_new = rotate(qkv[:, 1].reshape(local_rows, heads_here, HS), positions).astype(jnp.bfloat16)
    value_new = qkv[:, 2].reshape(local_rows, heads_here, HS).astype(jnp.bfloat16)
    scale = 1.0 / math.sqrt(HS)
    longest = prefix_keys.shape[1]
    own_count = own_keys.shape[1]
    grouped = query.reshape(groups_here, GSIZE, heads_here, HS)
    pre_keys = prefix_keys.reshape(groups_here, longest, heads_here, HS)
    pre_vals = prefix_values.reshape(groups_here, longest, heads_here, HS)
    mine_keys = own_keys.reshape(local_rows, own_count, heads_here, HS)
    mine_vals = own_values.reshape(local_rows, own_count, heads_here, HS)
    pre_scores = (
        jnp.einsum("gqhd,gjhd->gqhj", grouped, pre_keys, preferred_element_type=jnp.float32) * scale
    )
    pre_scores = jnp.where(
        jnp.arange(longest)[None, None, None, :] < prompt_len[:, None, None, None],
        pre_scores,
        -jnp.inf,
    )
    own_scores = (
        jnp.einsum("rhd,rthd->rht", query, mine_keys, preferred_element_type=jnp.float32) * scale
    )
    own_scores = jnp.where(
        jnp.arange(own_count)[None, None, :] < own_len[:, None, None], own_scores, -jnp.inf
    )
    self_scores = (
        jnp.einsum("rhd,rhd->rh", query, key_new, preferred_element_type=jnp.float32) * scale
    )
    pre_peak = jnp.max(pre_scores, axis=-1).reshape(local_rows, heads_here)
    peak = jnp.maximum(jnp.maximum(pre_peak, jnp.max(own_scores, axis=-1)), self_scores)
    pre_exp = jnp.exp(pre_scores - peak.reshape(groups_here, GSIZE, heads_here)[..., None])
    own_exp = jnp.exp(own_scores - peak[..., None])
    self_exp = jnp.exp(self_scores - peak)
    denom = (
        jnp.sum(pre_exp, axis=-1).reshape(local_rows, heads_here)
        + jnp.sum(own_exp, axis=-1)
        + self_exp
    )
    mixed = jnp.einsum(
        "gqhj,gjhd->gqhd",
        pre_exp.astype(jnp.bfloat16),
        pre_vals,
        preferred_element_type=jnp.float32,
    )
    mixed = mixed.reshape(local_rows, heads_here, HS)
    mixed = mixed + jnp.einsum(
        "rht,rthd->rhd", own_exp.astype(jnp.bfloat16), mine_vals, preferred_element_type=jnp.float32
    )
    mixed = mixed + self_exp.astype(jnp.bfloat16).astype(jnp.float32)[..., None] * value_new.astype(
        jnp.float32
    )
    attended = (mixed / denom[..., None]).astype(jnp.bfloat16)
    transposed = jnp.transpose(attended, (2, 1, 0))
    slices = lax.all_to_all(transposed, "grp", split_axis=0, concat_axis=2, tiled=True)
    dim_here = slices.shape[0]
    hidden = jax.nn.gelu(
        jnp.dot(
            lax.all_gather(normed, "grp", axis=0, tiled=True),
            w_in,
            preferred_element_type=jnp.float32,
        )
        + b_in.astype(jnp.float32),
        approximate=True,
    ).astype(jnp.bfloat16)
    units = hidden.shape[1]
    mlp_part = jnp.einsum(
        "gri,ihf->ghrf",
        hidden.reshape(grp_count, local_rows, units),
        w_down.reshape(units, head_count, width_here),
        preferred_element_type=jnp.float32,
    )
    attn_part = jnp.einsum(
        "dkgr,dkhf->ghrf",
        slices.reshape(dim_here, heads_here, grp_count, local_rows),
        w_attn_out.reshape(dim_here, heads_here, head_count, width_here),
        preferred_element_type=jnp.float32,
    )
    combined = (mlp_part + attn_part).reshape(grp_count * head_count * local_rows, width_here)
    summed = lax.psum_scatter(combined, ("grp", "head"), scatter_dimension=0, tiled=True)
    total = activations.astype(jnp.float32) + b_down.astype(jnp.float32)[None, :] + summed
    return total.astype(jnp.bfloat16)


def solution(mesh):
    in_specs = (
        P("grp", "head"),
        P(),
        P(),
        P("grp", None, "head"),
        P("grp", None, "head"),
        P("grp", None, "head"),
        P("grp", None, "head"),
        P("grp", None, "head"),
        P("grp"),
        P("grp"),
        P("grp", "head", None),
        P(None, ("grp", "head")),
        P(("grp", "head")),
        P(("grp", "head"), None),
        P("head"),
    )
    out_specs = P("grp", "head")
    return jax.shard_map(local, mesh=mesh, in_specs=in_specs, out_specs=out_specs, check_vma=False)
```

profile of v0, /device:TPU:0, one launch (start us, length us, event | category | flops | bytes accessed | tf_op | source)
XLA Modules:
  0.0 312.7 jit_solution(8511302075352348275)
XLA Ops:
  6.5 7.5 %all_gather.6 = bf16[32,4096]{1,0:T(8,128)(2,1)S(1)} all-gather(bf16[32,1024]{1,0:T(8,128)(2,1)} %param.15), channel_id=1, replica_groups=mesh['grp'=8,'head'=4] {'head'}, dimensions={1}, use_global_device_ids=true | all-gather | bytes 327680 | tf_op jit(solution)/shard_map/all_gather | solution.py:57
  16.1 15.1 %all_to_all.34 = bf16[32,8,512]{2,0,1:T(8,128)(2,1)S(1)} all-to-all(bf16[32,8,512]{2,0,1:T(8,128)(2,1)S(1)} %bitcast.125), channel_id=1, replica_groups=mesh['grp'=8,'head'=4] {'grp'}, dimensions={1} | all-to-all | bytes 524288 | tf_op jit(solution)/shard_map/all_to_all | solution.py:61
  31.2 2.2 convolution_convert_fusion
  36.2 2.7 reshape.209
  39.6 58.4 %reduce-scatter.3.cloned.1.call-done = bf16[32,3,1024]{2,0,1:T(8,128)(2,1)} async-done(((bf16[256,3,1024]{2,0,1:T(8,128)(2,1)}), bf16[32,3,1024]{2,0,1:T(8,128)(2,1)}) %reduce-scatter.3.cloned.1.call-update) | async-done | bytes 196624 | tf_op jit(solution)/shard_map/reduce_scatter | solution.py:62
  100.7 0.9 multiply_subtract_fusion
  103.5 0.9 subtract_convert_fusion
  105.6 1.1 multiply_reduce_fusion
  106.8 4.3 %fusion.65 = (f32[2,16,4]{1,2,0:T(4,128)S(1)}, f32[2,16,4,1024]{3,1,2,0:T(8,128)}) fusion(bf16[2,128,4,8,256]{4,3,2,1,0:T(8,128)(2,1)} %bitcast.120, bf16[2,16,4,64]{3,1,2,0:T(8,128)(2,1)S(1)} %copy.67, pred[2,1024]{1,0:T(4,128)(4,1)} %iota_compare_fusion.1, bf16[2,16,4,192]{3,1,0,2:T(8,128)(2,1)S(1)} %bitcast.126), kind=kOutput, calls=%fused_computation.98 | convolution fusion | flops 67633024 | bytes 4786688 | tf_op jit(solution)/shard_map/gqhd,gjhd->gqhj/dot_general | solution.py:86
  111.2 2.2 fusion.11
  114.3 1.3 fusion.42
  116.3 3.1 fusion.23
  120.3 1.0 fusion.56
  122.0 2.0 fusion.8
  124.3 0.9 reshape.224
  125.2 3.5 %all-to-all-start.1 = ((bf16[8,2,2048]{2,1,0:T(2,128)(2,1)}), bf16[8,2,2048]{2,1,0:T(2,128)(2,1)S(1)}, u32[]{:S(2)}, u32[]{:S(2)}) async-start(bf16[8,2,2048]{2,1,0:T(2,128)(2,1)} %reshape.224), calls=%async_computation.2 | async-start | bytes 131072 | tf_op jit(solution)/shard_map/all_to_all | solution.py:127
  128.7 20.8 %all-gather.2.cloned.1.call-done = bf16[256,4096]{1,0:T(8,128)(2,1)} async-done(((bf16[32,4096]{1,0:T(8,128)(2,1)}), bf16[256,4096]{1,0:T(8,128)(2,1)}) %all-gather.2.cloned.1.call-update) | async-done | bytes 2097168 | tf_op jit(solution)/shard_map/all_gather | solution.py:131
  149.5 4.4 %fusion.41 = bf16[256,512]{1,0:T(8,128)(2,1)S(1)} fusion(bf16[256,4096]{1,0:T(8,128)(2,1)} %all-gather.2.cloned.1.call-done, bf16[4096,512]{1,0:T(8,128)(2,1)} %param.26, f32[512]{0:T(512)} %convert_element_type.68), kind=kOutput, calls=%fused_computation.40 | convolution fusion | flops 1075052544 | bytes 6555648 | tf_op jit(solution)/shard_map/dot_general | solution.py:130
  153.9 3.2 %fusion.6 = f32[8,32,4,1024]{3,1,2,0:T(8,128)} fusion(bf16[8,32,512,1]{2,1,3,0:T(8,128)(2,1)S(1)} %bitcast.135, bf16[64,4,8,1024]{3,2,1,0:T(8,128)(2,1)S(1)} %bitcast.132), kind=kOutput, calls=%fused_computation.7 | convolution fusion | flops 1073741824 | bytes 8650752 | tf_op jit(solution)/shard_map/gri,ihf->ghrf/dot_general | solution.py:139
  157.1 0.9 reshape.225
  158.0 1.1 copy.81
  159.1 6.1 %bitcast_add_fusion = f32[8,32,4,1024]{3,1,2,0:T(8,128)} fusion(f32[8,32,4,1024]{3,1,2,0:T(8,128)} %fusion.6, bf16[32,4,4,1024]{3,2,1,0:T(4,128)(2,1)} %reshape.209, bf16[8,32,4,32]{1,3,2,0:T(8,128)(2,1)S(1)} %copy.81), kind=kOutput, calls=%fused_computation.9 | convolution fusion | flops 269484032 | bytes 9502720 | tf_op jit(solution)/shard_map/dkgr,dkhf->ghrf/dot_general | solution.py:145
  165.9 138.8 %reduce-scatter.5.cloned.1.call-done = f32[32,1024]{1,0:T(8,128)} async-done(((f32[1024,1024]{1,0:T(8,128)}), f32[32,1024]{1,0:T(8,128)}) %reduce-scatter.5.cloned.1.call-update) | async-done | bytes 131088 | tf_op jit(solution)/shard_map/reduce_scatter | solution.py:152
  304.7 1.6 add_convert_fusion
  (76 shorter events, 15.6 us)
Async XLA Ops:
  6.5 24.7 %copy-start = (bf16[512,3,1024]{2,0,1:T(8,128)(2,1)S(1)}, bf16[512,3,1024]{2,0,1:T(8,128)(2,1)}, u32[]{:S(2)}) copy-start(bf16[512,3,1024]{2,0,1:T(8,128)(2,1)} %param.18) | copy-start | bytes 9437188
  6.5 91.5 %reduce-scatter.3.cloned.1.call-start = ((), (), s32[]{:S(2)}) async-start(), calls=%async_computation.5 | async-start | bytes 1769472 | tf_op jit(solution)/shard_map/reduce_scatter | solution.py:62
  15.9 18.3 %copy-start.7 = (s32[2]{0:T(128)S(1)}, s32[2]{0:T(128)}, u32[]{:S(2)}) copy-start(s32[2]{0:T(128)} %param.23) | copy-start | bytes 28
  15.9 19.1 %copy-start.8 = (s32[32]{0:T(128)S(1)}, s32[32]{0:T(128)}, u32[]{:S(2)}) copy-start(s32[32]{0:T(128)} %param.24) | copy-start | bytes 388
  15.9 19.7 %copy-start.6 = (bf16[512]{0:T(512)(128)(2,1)S(1)}, bf16[512]{0:T(512)(128)(2,1)}, u32[]{:S(2)}) copy-start(bf16[512]{0:T(512)(128)(2,1)} %param.27) | copy-start | bytes 3076
  16.1 17.4 %copy-start.1 = (bf16[32,4096]{1,0:T(8,128)(2,1)}, bf16[32,4096]{1,0:T(8,128)(2,1)S(1)}, u32[]{:S(2)}) copy-start(bf16[32,4096]{1,0:T(8,128)(2,1)S(1)} %fusion.33) | copy-start | bytes 786436
  33.4 116.1 %all-gather.2.cloned.1.call-start = ((), (), s32[]{:S(2)}) async-start(), calls=%async_computation.4 | async-start | bytes 2359296 | tf_op jit(solution)/shard_map/all_gather | solution.py:131
  104.7 9.4 %copy-start.4 = (pred[32,32]{1,0:T(8,128)(4,1)S(1)}, pred[32,32]{1,0:T(8,128)(4,1)}, u32[]{:S(2)}) copy-start(pred[32,32]{1,0:T(8,128)(4,1)} %iota_compare_fusion) | copy-start | bytes 3076
  113.5 0.6 copy-start.3
  125.2 31.9 %all-to-all-start.1 = ((bf16[8,2,2048]{2,1,0:T(2,128)(2,1)}), bf16[8,2,2048]{2,1,0:T(2,128)(2,1)S(1)}, u32[]{:S(2)}, u32[]{:S(2)}) async-start(bf16[8,2,2048]{2,1,0:T(2,128)(2,1)} %reshape.224), calls=%async_computation.2 | async-start | bytes 131072 | tf_op jit(solution)/shard_map/all_to_all | solution.py:127
  128.7 176.0 %reduce-scatter.5.cloned.1.call-start = ((), (), s32[]{:S(2)}) async-start(), calls=%async_computation.6 | async-start | bytes 4325376 | tf_op jit(solution)/shard_map/reduce_scatter | solution.py:152
  149.5 4.4 %copy-start.9 = (bf16[512,4096]{1,0:T(8,128)(2,1)S(1)}, bf16[512,4096]{1,0:T(8,128)(2,1)}, u32[]{:S(2)}) copy-start(bf16[512,4096]{1,0:T(8,128)(2,1)} %param.28) | copy-start | bytes 12582916
  165.2 0.7 copy-start.5
  165.2 139.4 %copy-start.2 = (bf16[32,1024]{1,0:T(8,128)(2,1)S(1)}, bf16[32,1024]{1,0:T(8,128)(2,1)}, u32[]{:S(2)}) copy-start(bf16[32,1024]{1,0:T(8,128)(2,1)} %param.15) | copy-start | bytes 196612
Sparse Core Ops, SparseCore 0:
  33.5 64.4 reduce-scatter.2
  100.4 49.0 all-gather.1
  165.4 139.2 reduce-scatter.4
where the time goes:
time: 314 us; the launch traced here: 313 us
  waiting for transfers between devices  219 us (70%)
  matrix products  27.5 us (9%)
  blocking collectives  22.6 us (7%)
  other arithmetic  14.4 us (5%)
  between operations  13.3 us (4%)
  local copies, waits for them, and re-layouts  12.7 us (4%)
  starting transfers between devices  3.61 us (1%)
    reduce_scatter x1, waiting for transfers between devices, local(): lax.psum_scatter(combined, ('grp', 'head'), scatter_dimension=0, tiled=True)  139 us
    reduce_scatter x1, waiting for transfers between devices, local(): lax.psum_scatter(jnp.einsum('rf,fch->rch', columns, w_qkv, preferred_elem...  58.4 us
    all_gather x1, waiting for transfers between devices, local(): lax.all_gather(normed, 'grp', axis=0, tiled=True)  20.8 us
    all_to_all x1, blocking collectives, local(): lax.all_to_all(normed, 'grp', split_axis=1, concat_axis=0, tiled=True)  15.1 us
    all_gather x1, blocking collectives, local(): full_rows = lax.all_gather(activations, 'head', axis=1, tiled=True)  7.52 us
  transfers between devices with their start and end apart: 4, of which 3 were waited for; matrix products, arithmetic and copies ran while one was open for 13% of the time, Pallas kernels for 0%

commit v1 on v0

--- a/solution.py
+++ b/solution.py
@@ -1,22 +1,274 @@
+import functools
 import math
 
 import jax
 import jax.numpy as jnp
 from jax import lax
+from jax.experimental import pallas as pl
+from jax.experimental.pallas import tpu as pltpu
 from jax.sharding import PartitionSpec as P
 
 HS = 256
 ROT = 64
 GSIZE = 16
-
-
-def normalize(rows, gain, shift):
-    floats = rows.astype(jnp.float32)
+MESH = pl.DeviceIdType.MESH
+DMA = pltpu.SemaphoreType.DMA
+VMEM_SPEC = pl.BlockSpec(memory_space=pltpu.VMEM)
+VMEM_LIMIT = 56 * 1024 * 1024
+
+
+def remote(src, dst, send_sem, recv_sem, device):
+    return pltpu.make_async_remote_copy(
+        src_ref=src,
+        dst_ref=dst,
+        send_sem=send_sem,
+        recv_sem=recv_sem,
+        device_id=device,
+        device_id_type=MESH,
+    )
+
+
+def greet(devices):
+    barrier = pltpu.get_barrier_semaphore()
+    for device in devices:
+        pl.semaphore_signal(barrier, inc=1, device_id=device, device_id_type=MESH)
+    pl.semaphore_wait(barrier, len(devices))
+
+
+def place(zs):
+    g = lax.axis_index("grp")
+    h = lax.axis_index("head")
+    return g, h, g // 2, g % 2, h // 2, h % 2
+
+
+def gather_kernel(zs, heads, act, gain, shift, out, full, hs, hr, zsend, zr, ys, yr, xs, xr, cs, cr, ds_, dr):
+    g, h, z, y, x, c = place(zs)
+    rows, width = act.shape
+    xh = (1 - x) * 2 + c
+    ch = x * 2 + (1 - c)
+    yg = z * 2 + (1 - y)
+    peers = [(g, lax.rem(h + k, heads)) for k in range(1, heads)]
+    zpeers = [(lax.rem(z + k, zs) * 2 + y, h) for k in range(1, zs)]
+    greet(peers + zpeers + [(yg, h)])
+
+    def columns(ref, quarter):
+        return ref.at[:, pl.ds(pl.multiple_of(quarter * width, 128), width)]
+
+    def piece(group, quarter):
+        return out.at[
+            pl.ds(pl.multiple_of(group * rows, 32), rows),
+            pl.ds(pl.multiple_of(quarter * width, 128), width),
+        ]
+
+    started = []
+
+    def start(copy):
+        copy.start()
+        started.append(copy)
+
+    for k in range(1, heads):
+        start(remote(act, columns(full, h), hs.at[k], hr.at[k], peers[k - 1]))
+    full[:, pl.ds(pl.multiple_of(h * width, 128), width)] = act[...]
+    for k in range(1, heads):
+        origin = lax.rem(h + heads - k, heads)
+        remote(act, columns(full, origin), hs.at[k], hr.at[k], peers[k - 1]).wait_recv()
+    floats = full[...].astype(jnp.float32)
     center = floats - jnp.mean(floats, axis=-1, keepdims=True)
     spread = jnp.mean(center * center, axis=-1, keepdims=True)
-    return (
-        center * lax.rsqrt(spread + 1e-05) * gain.astype(jnp.float32) + shift.astype(jnp.float32)
-    ).astype(jnp.bfloat16)
+    normed = center * lax.rsqrt(spread + 1e-05) * gain[...].astype(jnp.float32) + shift[...].astype(
+        jnp.float32
+    )
+    out[pl.ds(pl.multiple_of(g * rows, 32), rows), :] = normed.astype(jnp.bfloat16)
+
+    for k in range(1, zs):
+        start(remote(piece(g, h), piece(g, h), zsend.at[k], zr.at[k], zpeers[k - 1]))
+    start(remote(piece(g, h), piece(g, h), ys.at[0], yr.at[0], (yg, h)))
+
+    def spread_out(i, group):
+        start(remote(piece(group, h), piece(group, h), xs.at[i], xr.at[i], (g, xh)))
+        start(remote(piece(group, h), piece(group, h), cs.at[i], cr.at[i], (g, ch)))
+
+    order = []
+    for j in range(zs):
+        if j > 0:
+            group = lax.rem(z + zs - j, zs) * 2 + y
+            remote(piece(group, h), piece(group, h), zsend.at[j], zr.at[j], zpeers[j - 1]).wait_recv()
+            start(remote(piece(group, h), piece(group, h), ys.at[j], yr.at[j], (yg, h)))
+            spread_out(2 * j, group)
+            order.append((2 * j, group))
+        group = lax.rem(z + zs - j, zs) * 2 + (1 - y)
+        remote(piece(group, h), piece(group, h), ys.at[j], yr.at[j], (yg, h)).wait_recv()
+        spread_out(2 * j + 1, group)
+        order.append((2 * j + 1, group))
+    order.sort(key=lambda entry: entry[0] if entry[0] % 2 else entry[0])
+    for i, group in order:
+        remote(piece(group, xh), piece(group, xh), xs.at[i], xr.at[i], (g, xh)).wait_recv()
+        start(remote(piece(group, xh), piece(group, xh), ds_.at[i], dr.at[i], (g, ch)))
+    for i, group in order:
+        other = (1 - x) * 2 + (1 - c)
+        remote(piece(group, ch), piece(group, ch), cs.at[i], cr.at[i], (g, ch)).wait_recv()
+        remote(piece(group, other), piece(group, other), ds_.at[i], dr.at[i], (g, ch)).wait_recv()
+    for copy in started:
+        copy.wait_send()
+
+
+def gather_normed(activations, gain, shift):
+    groups, heads = lax.axis_size("grp"), lax.axis_size("head")
+    zs = groups // 2
+    rows, width = activations.shape
+    scratch = [pltpu.VMEM((rows, width * heads), jnp.bfloat16)]
+    scratch += [DMA((heads,))] * 2 + [DMA((zs,))] * 4 + [DMA((groups,))] * 6
+    return pl.pallas_call(
+        functools.partial(gather_kernel, zs, heads),
+        out_shape=jax.ShapeDtypeStruct((groups * rows, heads * width), jnp.bfloat16),
+        in_specs=[VMEM_SPEC] * 3,
+        out_specs=VMEM_SPEC,
+        scratch_shapes=scratch,
+        compiler_params=pltpu.CompilerParams(
+            collective_id=0, has_side_effects=True, vmem_limit_bytes=VMEM_LIMIT
+        ),
+        name="gather_normed",
+    )(activations, gain.reshape(1, -1), shift.reshape(1, -1))
+
+
+def qkv_kernel(zs, part, out, r3, s4, r4, ys, yr, zsend, zr):
+    g, h, z, y, x, c = place(zs)
+    rows = out.shape[1]
+    yg = z * 2 + (1 - y)
+    zpeers = [(lax.rem(z + k, zs) * 2 + y, h) for k in range(1, zs)]
+    greet(zpeers + [(yg, h)])
+
+    def block(k, side):
+        group = lax.rem(z + k, zs) * 2 + side
+        return pl.ds(pl.multiple_of(group * rows, 32), rows)
+
+    turns = list(range(1, zs)) + [0]
+    ycopies = {}
+    for k in turns:
+        ycopies[k] = remote(part.at[:, block(k, 1 - y), :], r3.at[k], ys.at[k], yr.at[k], (yg, h))
+        ycopies[k].start()
+    zcopies = []
+    for k in range(1, zs):
+        ycopies[k].wait_recv()
+        pair = part[:, block(k, y), :].astype(jnp.float32) + r3[k].astype(jnp.float32)
+        s4[k] = pair.astype(jnp.bfloat16)
+        copy = remote(s4.at[k], r4.at[k], zsend.at[k], zr.at[k], zpeers[k - 1])
+        copy.start()
+        zcopies.append(copy)
+    ycopies[0].wait_recv()
+    total = part[:, block(0, y), :].astype(jnp.float32) + r3[0].astype(jnp.float32)
+    for k in range(1, zs):
+        zcopies[k - 1].wait_recv()
+        total = total + r4[k].astype(jnp.float32)
+    out[...] = total
+    for k in turns:
+        ycopies[k].wait_send()
+    for copy in zcopies:
+        copy.wait_send()
+
+
+def qkv_scatter(part):
+    groups = lax.axis_size("grp")
+    zs = groups // 2
+    rows, width = part.shape[1] // groups, part.shape[2]
+    buffer = pltpu.VMEM((zs, 3, rows, width), jnp.bfloat16)
+    return pl.pallas_call(
+        functools.partial(qkv_kernel, zs),
+        out_shape=jax.ShapeDtypeStruct((3, rows, width), jnp.float32),
+        in_specs=[VMEM_SPEC],
+        out_specs=VMEM_SPEC,
+        scratch_shapes=[buffer] * 3 + [DMA((zs,))] * 4,
+        compiler_params=pltpu.CompilerParams(
+            collective_id=1, has_side_effects=True, vmem_limit_bytes=VMEM_LIMIT
+        ),
+        name="qkv_scatter",
+    )(part)
+
+
+def out_kernel(zs, part, act, b_down, out, s1, r1, s2, r2, s3, r3, s4, r4, cs, cr, xs, xr, ys, yr, zsend, zr):
+    g, h, z, y, x, c = place(zs)
+    rows, width = act.shape
+    xh = (1 - x) * 2 + c
+    ch = x * 2 + (1 - c)
+    yg = z * 2 + (1 - y)
+    zpeers = [(lax.rem(z + k, zs) * 2 + y, h) for k in range(1, zs)]
+    greet(zpeers + [(yg, h), (g, xh), (g, ch)])
+
+    def term(k, ky, quarter):
+        side = 1 - y if ky else y
+        group = lax.rem(z + k, zs) * 2 + side
+        return part[
+            pl.ds(pl.multiple_of(group * rows, 32), rows),
+            pl.ds(pl.multiple_of(quarter * width, 128), width),
+        ]
+
+    turns = list(range(1, zs)) + [0]
+    order = [(k, 1) for k in turns] + [(k, 0) for k in turns]
+    sends = []
+    ccopy, xcopy, ycopy, zcopy = {}, {}, {}, {}
+    for k, ky in order:
+        i = 2 * k + ky
+        s1[i, 0] = term(k, ky, 1 - c).astype(jnp.bfloat16)
+        s1[i, 1] = term(k, ky, 3 - c).astype(jnp.bfloat16)
+        ccopy[i] = remote(s1.at[i], r1.at[i], cs.at[i], cr.at[i], (g, ch))
+        ccopy[i].start()
+    for k, ky in order:
+        i = 2 * k + ky
+        ccopy[i].wait_recv()
+        s2[i] = (term(k, ky, xh) + r1[i, 1 - x].astype(jnp.float32)).astype(jnp.bfloat16)
+        xcopy[i] = remote(s2.at[i], r2.at[i], xs.at[i], xr.at[i], (g, xh))
+        xcopy[i].start()
+
+    def chip_sum(k, ky):
+        i = 2 * k + ky
+        xcopy[i].wait_recv()
+        return term(k, ky, h) + r1[i, x].astype(jnp.float32) + r2[i].astype(jnp.float32)
+
+    for k in turns:
+        s3[k] = chip_sum(k, 1).astype(jnp.bfloat16)
+        ycopy[k] = remote(s3.at[k], r3.at[k], ys.at[k], yr.at[k], (yg, h))
+        ycopy[k].start()
+    for k in range(1, zs):
+        total = chip_sum(k, 0)
+        ycopy[k].wait_recv()
+        s4[k] = (total + r3[k].astype(jnp.float32)).astype(jnp.bfloat16)
+        zcopy[k] = remote(s4.at[k], r4.at[k], zsend.at[k], zr.at[k], zpeers[k - 1])
+        zcopy[k].start()
+    total = chip_sum(0, 0) + act[...].astype(jnp.float32) + b_down[...].astype(jnp.float32)
+    ycopy[0].wait_recv()
+    total = total + r3[0].astype(jnp.float32)
+    for k in range(1, zs):
+        zcopy[k].wait_recv()
+        total = total + r4[k].astype(jnp.float32)
+    out[...] = total.astype(jnp.bfloat16)
+    for copies in (ccopy, xcopy, ycopy, zcopy):
+        for copy in copies.values():
+            copy.wait_send()
+
+
+def out_scatter(part, activations, b_down):
+    groups = lax.axis_size("grp")
+    zs = groups // 2
+    rows, width = activations.shape
+
+    def buffer(*lead):
+        return pltpu.VMEM(lead + (rows, width), jnp.bfloat16)
+
+    return pl.pallas_call(
+        functools.partial(out_kernel, zs),
+        out_shape=jax.ShapeDtypeStruct((rows, width), jnp.bfloat16),
+        in_specs=[VMEM_SPEC] * 3,
+        out_specs=VMEM_SPEC,
+        scratch_shapes=[buffer(groups, 2)] * 2
+        + [buffer(groups)] * 2
+        + [buffer(zs)] * 4
+        + [DMA((groups,))] * 4
+        + [DMA((zs,))] * 4,
+        compiler_params=pltpu.CompilerParams(
+            collective_id=2, has_side_effects=True, vmem_limit_bytes=VMEM_LIMIT
+        ),
+        name="out_scatter",
+    )(part, activations, b_down.reshape(1, -1))
 
 
 def rotate(values, positions):
@@ -54,26 +306,25 @@
     grp_count = lax.axis_size("grp")
     head_count = lax.axis_size("head")
     width_here = activations.shape[1]
-    full_rows = lax.all_gather(activations, "head", axis=1, tiled=True)
-    normed = normalize(full_rows, ln_gain, ln_bias)
-    local_rows = normed.shape[0]
+    local_rows = activations.shape[0]
     groups_here = prompt_len.shape[0]
-    columns = lax.all_to_all(normed, "grp", split_axis=1, concat_axis=0, tiled=True)
-    qkv = lax.psum_scatter(
-        jnp.einsum("rf,fch->rch", columns, w_qkv, preferred_element_type=jnp.float32).astype(
+    gathered = gather_normed(activations, ln_gain, ln_bias)
+    features = w_qkv.shape[0]
+    columns = lax.dynamic_slice_in_dim(
+        gathered, lax.axis_index("grp") * features, features, axis=1
+    )
+    qkv = qkv_scatter(
+        jnp.einsum("rf,fch->crh", columns, w_qkv, preferred_element_type=jnp.float32).astype(
             jnp.bfloat16
-        ),
-        "grp",
-        scatter_dimension=0,
-        tiled=True,
-    ).astype(jnp.float32)
+        )
+    )
     heads_here = w_qkv.shape[2] // HS
     member = (jnp.arange(local_rows) // GSIZE)[:, None] == jnp.arange(groups_here)[None, :]
     row_prompt = jnp.sum(jnp.where(member, prompt_len[None, :], 0), axis=1)
     positions = (row_prompt + own_len).astype(jnp.float32)
-    query = rotate(qkv[:, 0].reshape(local_rows, heads_here, HS), positions).astype(jnp.bfloat16)
-    key_new = rotate(qkv[:, 1].reshape(local_rows, heads_here, HS), positions).astype(jnp.bfloat16)
-    value_new = qkv[:, 2].reshape(local_rows, heads_here, HS).astype(jnp.bfloat16)
+    query = rotate(qkv[0].reshape(local_rows, heads_here, HS), positions).astype(jnp.bfloat16)
+    key_new = rotate(qkv[1].reshape(local_rows, heads_here, HS), positions).astype(jnp.bfloat16)
+    value_new = qkv[2].reshape(local_rows, heads_here, HS).astype(jnp.bfloat16)
     scale = 1.0 / math.sqrt(HS)
     longest = prefix_keys.shape[1]
     own_count = own_keys.shape[1]
@@ -128,30 +379,22 @@
     dim_here = slices.shape[0]
     hidden = jax.nn.gelu(
         jnp.dot(
-            lax.all_gather(normed, "grp", axis=0, tiled=True),
+            gathered,
             w_in,
             preferred_element_type=jnp.float32,
         )
         + b_in.astype(jnp.float32),
         approximate=True,
     ).astype(jnp.bfloat16)
-    units = hidden.shape[1]
-    mlp_part = jnp.einsum(
-        "gri,ihf->ghrf",
-        hidden.reshape(grp_count, local_rows, units),
-        w_down.reshape(units, head_count, width_here),
+    attn_rows = jnp.transpose(
+        slices.reshape(dim_here * heads_here, grp_count * local_rows), (1, 0)
+    )
+    combined = jnp.dot(hidden, w_down, preferred_element_type=jnp.float32) + jnp.dot(
+        attn_rows,
+        w_attn_out.reshape(dim_here * heads_here, head_count * width_here),
         preferred_element_type=jnp.float32,
     )
-    attn_part = jnp.einsum(
-        "dkgr,dkhf->ghrf",
-        slices.reshape(dim_here, heads_here, grp_count, local_rows),
-        w_attn_out.reshape(dim_here, heads_here, head_count, width_here),
-        preferred_element_type=jnp.float32,
-    )
-    combined = (mlp_part + attn_part).reshape(grp_count * head_count * local_rows, width_here)
-    summed = lax.psum_scatter(combined, ("grp", "head"), scatter_dimension=0, tiled=True)
-    total = activations.astype(jnp.float32) + b_down.astype(jnp.float32)[None, :] + summed
-    return total.astype(jnp.bfloat16)
+    return out_scatter(combined, activations, b_down)
 
 
 def solution(mesh):

time: 314 us -> 145 us (0.46)
  waiting for transfers between devices: 219 us -> 2.78 us
  Pallas kernels: 0 us -> 81.6 us
  blocking collectives: 22.6 us -> 0 us
  between operations: 13.3 us -> 0.26 us
  local copies, waits for them, and re-layouts: 12.7 us -> 16.3 us
  other arithmetic: 14.4 us -> 11.1 us
    reduce_scatter x2 -> x0, waiting for transfers between devices: 197 us -> none  [the longest x1 139 us: local(): lax.psum_scatter(combined, ('grp', 'head'), scatter_dimension=0, tiled=True)]
    pallas_call x0 -> x3, Pallas kernels: none -> 81.6 us  [the longest x1 31.1 us: gather_normed(): pl.pallas_call(functools.partial(gather_kernel, zs, heads), out_shape=jax...]
    all_gather x1 -> x0, waiting for transfers between devices: 20.8 us -> none  [local(): lax.all_gather(normed, 'grp', axis=0, tiled=True)]
    all_to_all x1 -> x0, blocking collectives: 15.1 us -> none  [local(): lax.all_to_all(normed, 'grp', split_axis=1, concat_axis=0, tiled=True)]
    all_gather x1 -> x0, blocking collectives: 7.52 us -> none  [local(): full_rows = lax.all_gather(activations, 'head', axis=1, tiled=True)]
    reshape x1 -> x5, local copies, waits for them, and re-layouts: 2.66 us -> 7.51 us  [the longest x1 2.17 us: local(): w_attn_out.reshape(dim_here * heads_here, head_count * width_here)]
    dot_general x4 -> x3, matrix products: 15.9 us -> 16.7 us  [the longest x1 9.74 us: local(): jnp.dot(hidden, w_down, preferred_element_type=jnp.float32)]
  transfers between devices with their start and end apart: 4 -> 1, of which waited for: 3 -> 1; matrix products, arithmetic and copies ran while one was open for 13% -> 3% of each run, Pallas kernels for 0% -> 0%
where the time goes in v1:
time: 145 us; the launch traced here: 144 us
  Pallas kernels  81.6 us (56%)
  matrix products  28.2 us (19%)
  local copies, waits for them, and re-layouts  16.3 us (11%)
  other arithmetic  11.1 us (8%)
  starting transfers between devices  3.99 us (3%)
  waiting for transfers between devices  2.78 us (2%)
    pallas_call x1, Pallas kernels, gather_normed(): pl.pallas_call(functools.partial(gather_kernel, zs, heads), out_shape=jax...  31.1 us
    pallas_call x1, Pallas kernels, qkv_scatter(): pl.pallas_call(functools.partial(qkv_kernel, zs), out_shape=jax.ShapeDtyp...  28.1 us
    pallas_call x1, Pallas kernels, out_scatter(): pl.pallas_call(functools.partial(out_kernel, zs), out_shape=jax.ShapeDtyp...  22.4 us
    dot_general x1, matrix products, local(): jnp.dot(hidden, w_down, preferred_element_type=jnp.float32)  9.74 us
    dot_general x1, matrix products, local(): jnp.einsum('gqhd,gjhd->gqhj', grouped, pre_keys, preferred_element_type=j...  4.2 us
    all_to_all x1, starting transfers between devices, local(): lax.all_to_all(transposed, 'grp', split_axis=0, concat_axis=2, tiled=True)  3.99 us
    dot_general x1, matrix products, local(): jnp.dot(attn_rows, w_attn_out.reshape(dim_here * heads_here, head_count *...  3.88 us
    unnamed x16, local copies, waits for them, and re-layouts  3.63 us
  transfers between devices with their start and end apart: 1, of which 1 were waited for; matrix products, arithmetic and copies ran while one was open for 3% of the time, Pallas kernels for 0%

profile of v1, /device:TPU:0, one launch (start us, length us, event | category | flops | bytes accessed | tf_op | source)
XLA Modules:
  0.0 144.4 jit_solution(4299910300693248445)
XLA Ops:
  0.6 1.6 %reshape.180.gain = bf16[1,4096]{1,0:T(2,128)(2,1)} reshape(bf16[4096]{0:T(1024)(128)(2,1)} %param.16) | data formatting | bytes 16384 | tf_op jit(solution)/shard_map/reshape | solution.py:131
  2.1 1.3 reshape.181.shift
  3.4 31.1 %gather_normed.1 = bf16[256,4096]{1,0:T(8,128)(2,1)} custom-call(bf16[32,1024]{1,0:T(8,128)(2,1)} %act.3, bf16[1,4096]{1,0:T(2,128)(2,1)} %reshape.180.gain, bf16[1,4096]{1,0:T(2,128)(2,1)} %reshape.181.shift), custom_call_target="tpu_custom_call" | custom-call | tf_op jit(solution)/shard_map/gather_normed/pallas_call | solution.py:121
  34.6 3.1 %fusion.12.part = bf16[3,256,1024]{2,1,0:T(8,128)(2,1)} fusion(bf16[512,3,1024]{2,0,1:T(8,128)(2,1)S(1)} %copy-done, bf16[256,4096]{1,0:T(8,128)(2,1)} %gather_normed.1, s32[]{:T(128)S(6)} %select_n.27), kind=kOutput, calls=%fused_computation.14 | convolution fusion | flops 806092800 | bytes 4980740 | tf_op jit(solution)/shard_map/rf,fch->crh/dot_general | solution.py:317
  37.7 28.1 %qkv_scatter.1 = f32[3,32,1024]{2,1,0:T(8,128)} custom-call(bf16[3,256,1024]{2,1,0:T(8,128)(2,1)} %fusion.12.part), custom_call_target="tpu_custom_call" | custom-call | tf_op jit(solution)/shard_map/qkv_scatter/pallas_call | solution.py:175
  65.8 1.0 fusion.67
  74.9 1.1 multiply_reduce_fusion
  76.2 4.2 %fusion.68 = (f32[2,16,4]{1,2,0:T(4,128)S(1)}, f32[2,16,4,1024]{3,1,2,0:T(8,128)}) fusion(bf16[2,128,4,8,256]{4,3,2,1,0:T(8,128)(2,1)} %bitcast.87, bf16[2,16,4,64]{3,1,2,0:T(8,128)(2,1)S(1)} %copy.55, pred[2,1024]{1,0:T(4,128)(4,1)} %iota_compare_fusion.1, bf16[2,16,4,192]{3,1,0,2:T(8,128)(2,1)S(1)} %bitcast.91), kind=kOutput, calls=%fused_computation.95 | convolution fusion | flops 67633024 | bytes 4786688 | tf_op jit(solution)/shard_map/gqhd,gjhd->gqhj/dot_general | solution.py:337
  80.5 2.2 %fusion.9 = f32[32,4,1,32]{3,2,1,0:T(1,128)S(1)} fusion(bf16[32,4,4,8,256]{4,3,2,1,0:T(8,128)(2,1)} %bitcast.97, bf16[32,4,256,1]{2,0,1,3:T(8,128)(2,1)S(1)} %get-tuple-element.13), kind=kOutput, calls=%fused_computation.10 | convolution fusion | flops 2097152 | bytes 2179072 | tf_op jit(solution)/shard_map/rhd,rthd->rht/dot_general | solution.py:345
  82.9 1.3 fusion.54
  84.2 0.9 fusion.48
  85.2 1.3 fusion.33
  86.5 3.1 %fusion.22 = f32[2,16,4,256]{3,1,2,0:T(8,128)S(1)} fusion(bf16[2,128,4,8,256]{4,3,2,1,0:T(8,128)(2,1)} %bitcast.88, f32[2,16,4,1024]{3,1,2,0:T(8,128)} %get-tuple-element.20, f32[2,16,4]{1,2,0:T(4,128)S(1)} %copy.62), kind=kOutput, calls=%fused_computation.19 | convolution fusion | flops 67371008 | bytes 4850176 | tf_op jit(solution)/shard_map/gqhj,gjhd->gqhd/dot_general | solution.py:363
  90.4 2.0 %fusion.6 = f32[32,4,1,256]{3,2,1,0:T(1,128)S(1)} fusion(bf16[32,4,4,8,256]{4,3,2,1,0:T(8,128)(2,1)} %bitcast.98, bf16[32,4,32,1]{2,0,1,3:T(8,128)(2,1)} %get-tuple-element.16), kind=kOutput, calls=%fused_computation.7 | convolution fusion | flops 2097152 | bytes 2236416 | tf_op jit(solution)/shard_map/rht,rthd->rhd/dot_general | solution.py:370
  93.6 4.0 %all-to-all-start = ((bf16[8,2,2048]{2,1,0:T(2,128)(2,1)}), bf16[8,2,2048]{2,1,0:T(2,128)(2,1)S(1)}, u32[]{:S(2)}, u32[]{:S(2)}) async-start(bf16[8,2,2048]{2,1,0:T(2,128)(2,1)} %reshape.204), calls=%async_computation | async-start | bytes 131072 | tf_op jit(solution)/shard_map/all_to_all | solution.py:378
  97.6 2.2 %reshape.194 = bf16[128,4096]{1,0:T(8,128)(2,1)} reshape(bf16[32,4,4096]{2,1,0:T(4,128)(2,1)} %param.25) | data formatting | bytes 2097152 | tf_op jit(solution)/shard_map/reshape | solution.py:394
  100.4 1.3 reshape.195.b_down
  101.7 2.8 %all-to-all-done = bf16[8,2,2048]{2,1,0:T(2,128)(2,1)S(1)} async-done(((bf16[8,2,2048]{2,1,0:T(2,128)(2,1)}), bf16[8,2,2048]{2,1,0:T(2,128)(2,1)S(1)}, u32[]{:S(2)}, u32[]{:S(2)}) %all-to-all-start) | async-done | bytes 65568 | tf_op jit(solution)/shard_map/all_to_all | solution.py:378
  104.7 1.0 copy.136
  105.7 1.2 reshape.193
  106.8 3.9 %fusion.69 = f32[256,4096]{1,0:T(8,128)} fusion(bf16[128,256]{1,0:T(8,128)(2,1)S(1)} %reshape.193, bf16[128,4096]{1,0:T(8,128)(2,1)} %reshape.194), kind=kOutput, calls=%fused_computation.96 | convolution fusion | flops 268435456 | bytes 5308416 | tf_op jit(solution)/shard_map/dot_general | solution.py:392
  110.7 9.7 %convolution_add_fusion.part = f32[256,4096]{1,0:T(8,128)} fusion(f32[256,4096]{1,0:T(8,128)} %fusion.69, bf16[512,4096]{1,0:T(8,128)(2,1)} %param.28, bf16[256,4096]{1,0:T(8,128)(2,1)} %gather_normed.1, bf16[4096,512]{1,0:T(8,128)(2,1)} %param.26, f32[512]{0:T(512)S(1)} %convert_element_type.40), kind=kOutput, calls=%fused_computation | convolution fusion | flops 2149842944 | bytes 18876416 | tf_op jit(solution)/shard_map/dot_general | solution.py:392
  120.5 22.4 %out_scatter.1 = bf16[32,1024]{1,0:T(8,128)(2,1)} custom-call(f32[256,4096]{1,0:T(8,128)} %convolution_add_fusion.part, bf16[32,1024]{1,0:T(8,128)(2,1)} %act.3, bf16[1,1024]{1,0:T(2,128)(2,1)} %reshape.195.b_down), custom_call_target="tpu_custom_call" | custom-call | tf_op jit(solution)/shard_map/out_scatter/pallas_call | solution.py:257
  142.9 1.5 %copy.138 = bf16[32,1024]{1,0:T(8,128)(2,1)} copy(bf16[32,1024]{1,0:T(8,128)(2,1)} %out_scatter.1) | data formatting | bytes 131072
  (52 shorter events, 12.0 us)
Async XLA Ops:
  0.0 34.6 %copy-start = (bf16[512,3,1024]{2,0,1:T(8,128)(2,1)S(1)}, bf16[512,3,1024]{2,0,1:T(8,128)(2,1)}, u32[]{:S(2)}) copy-start(bf16[512,3,1024]{2,0,1:T(8,128)(2,1)} %param.18) | copy-start | bytes 9437188
  34.6 34.0 %copy-start.3 = (s32[2]{0:T(128)S(1)}, s32[2]{0:T(128)}, u32[]{:S(2)}) copy-start(s32[2]{0:T(128)} %param.23) | copy-start | bytes 28
  34.6 34.7 %copy-start.4 = (s32[32]{0:T(128)S(1)}, s32[32]{0:T(128)}, u32[]{:S(2)}) copy-start(s32[32]{0:T(128)} %param.24) | copy-start | bytes 388
  70.7 1.2 copy-start.1
  74.1 8.7 %copy-start.2 = (pred[32,32]{1,0:T(8,128)(4,1)S(1)}, pred[32,32]{1,0:T(8,128)(4,1)}, u32[]{:S(2)}) copy-start(pred[32,32]{1,0:T(8,128)(4,1)} %iota_compare_fusion) | copy-start | bytes 3076
  93.6 10.9 %all-to-all-start = ((bf16[8,2,2048]{2,1,0:T(2,128)(2,1)}), bf16[8,2,2048]{2,1,0:T(2,128)(2,1)S(1)}, u32[]{:S(2)}, u32[]{:S(2)}) async-start(bf16[8,2,2048]{2,1,0:T(2,128)(2,1)} %reshape.204), calls=%async_computation | async-start | bytes 131072 | tf_op jit(solution)/shard_map/all_to_all | solution.py:378

commit v2 on v1

--- a/solution.py
+++ b/solution.py
@@ -41,7 +41,7 @@
     return g, h, g // 2, g % 2, h // 2, h % 2
 
 
-def gather_kernel(zs, heads, act, gain, shift, out, full, hs, hr, zsend, zr, ys, yr, xs, xr, cs, cr, ds_, dr):
+def gather_kernel(zs, heads, act, affine, out, full, hs, hr, zsend, zr, ys, yr, xs, xr, cs, cr, ds_, dr):
     g, h, z, y, x, c = place(zs)
     rows, width = act.shape
     xh = (1 - x) * 2 + c
@@ -75,9 +75,7 @@
     floats = full[...].astype(jnp.float32)
     center = floats - jnp.mean(floats, axis=-1, keepdims=True)
     spread = jnp.mean(center * center, axis=-1, keepdims=True)
-    normed = center * lax.rsqrt(spread + 1e-05) * gain[...].astype(jnp.float32) + shift[...].astype(
-        jnp.float32
-    )
+    normed = center * lax.rsqrt(spread + 1e-05) * affine[0:1, :] + affine[1:2, :]
     out[pl.ds(pl.multiple_of(g * rows, 32), rows), :] = normed.astype(jnp.bfloat16)
 
     for k in range(1, zs):
@@ -121,14 +119,14 @@
     return pl.pallas_call(
         functools.partial(gather_kernel, zs, heads),
         out_shape=jax.ShapeDtypeStruct((groups * rows, heads * width), jnp.bfloat16),
-        in_specs=[VMEM_SPEC] * 3,
+        in_specs=[VMEM_SPEC] * 2,
         out_specs=VMEM_SPEC,
         scratch_shapes=scratch,
         compiler_params=pltpu.CompilerParams(
             collective_id=0, has_side_effects=True, vmem_limit_bytes=VMEM_LIMIT
         ),
         name="gather_normed",
-    )(activations, gain.reshape(1, -1), shift.reshape(1, -1))
+    )(activations, jnp.stack([gain, shift]).astype(jnp.float32))
 
 
 def qkv_kernel(zs, part, out, r3, s4, r4, ys, yr, zsend, zr):
@@ -185,19 +183,45 @@
     )(part)
 
 
-def out_kernel(zs, part, act, b_down, out, s1, r1, s2, r2, s3, r3, s4, r4, cs, cr, xs, xr, ys, yr, zsend, zr):
+def out_kernel(zs, part, att, w_out, out, acc, ra, asend, arecv, s1, r1, s2, r2, s3, r3, s4, r4, cs, cr, xs, xr, ys, yr, zsend, zr):
     g, h, z, y, x, c = place(zs)
-    rows, width = act.shape
+    rows, width = out.shape
     xh = (1 - x) * 2 + c
     ch = x * 2 + (1 - c)
     yg = z * 2 + (1 - y)
     zpeers = [(lax.rem(z + k, zs) * 2 + y, h) for k in range(1, zs)]
-    greet(zpeers + [(yg, h), (g, xh), (g, ch)])
+    groups = 2 * zs
+    gpeers = [lax.rem(g + k, groups) for k in range(1, groups)]
+    greet([(p, h) for p in gpeers] + [(g, xh), (g, ch)])
+
+    def rows_of(group):
+        return pl.ds(pl.multiple_of(group * rows, 32), rows)
+
+    acopies = []
+    for k in range(1, groups):
+        peer = gpeers[k - 1]
+        copy = remote(att.at[peer], ra.at[rows_of(g), :], asend.at[k], arecv.at[k], (peer, h))
+        copy.start()
+        acopies.append(copy)
+    ra[rows_of(g), :] = att[g]
+    for k in range(1, groups):
+        origin = lax.rem(g + groups - k, groups)
+        remote(
+            att.at[origin], ra.at[rows_of(origin), :], asend.at[k], arecv.at[k], (gpeers[k - 1], h)
+        ).wait_recv()
+    tile = 512
+
+    @pl.loop(0, part.shape[1] // tile)
+    def _(t):
+        columns = pl.ds(pl.multiple_of(t * tile, tile), tile)
+        acc[:, columns] = part[:, columns] + jnp.dot(
+            ra[...], w_out[:, columns], preferred_element_type=jnp.float32
+        )
 
     def term(k, ky, quarter):
         side = 1 - y if ky else y
         group = lax.rem(z + k, zs) * 2 + side
-        return part[
+        return acc[
             pl.ds(pl.multiple_of(group * rows, 32), rows),
             pl.ds(pl.multiple_of(quarter * width, 128), width),
         ]
@@ -234,32 +258,40 @@
         s4[k] = (total + r3[k].astype(jnp.float32)).astype(jnp.bfloat16)
         zcopy[k] = remote(s4.at[k], r4.at[k], zsend.at[k], zr.at[k], zpeers[k - 1])
         zcopy[k].start()
-    total = chip_sum(0, 0) + act[...].astype(jnp.float32) + b_down[...].astype(jnp.float32)
+    total = chip_sum(0, 0)
     ycopy[0].wait_recv()
     total = total + r3[0].astype(jnp.float32)
     for k in range(1, zs):
         zcopy[k].wait_recv()
         total = total + r4[k].astype(jnp.float32)
-    out[...] = total.astype(jnp.bfloat16)
+    out[...] = total
+    for copy in acopies:
+        copy.wait_send()
     for copies in (ccopy, xcopy, ycopy, zcopy):
         for copy in copies.values():
             copy.wait_send()
 
 
-def out_scatter(part, activations, b_down):
+def out_scatter(part, att, w_out, rows, width):
     groups = lax.axis_size("grp")
     zs = groups // 2
-    rows, width = activations.shape
+    everyone = groups * rows
 
     def buffer(*lead):
         return pltpu.VMEM(lead + (rows, width), jnp.bfloat16)
 
     return pl.pallas_call(
         functools.partial(out_kernel, zs),
-        out_shape=jax.ShapeDtypeStruct((rows, width), jnp.bfloat16),
+        out_shape=jax.ShapeDtypeStruct((rows, width), jnp.float32),
         in_specs=[VMEM_SPEC] * 3,
         out_specs=VMEM_SPEC,
-        scratch_shapes=[buffer(groups, 2)] * 2
+        scratch_shapes=[
+            pltpu.VMEM(part.shape, jnp.float32),
+            pltpu.VMEM((everyone, att.shape[2]), jnp.bfloat16),
+            DMA((groups,)),
+            DMA((groups,)),
+        ]
+        + [buffer(groups, 2)] * 2
         + [buffer(groups)] * 2
         + [buffer(zs)] * 4
         + [DMA((groups,))] * 4
@@ -268,22 +300,89 @@
             collective_id=2, has_side_effects=True, vmem_limit_bytes=VMEM_LIMIT
         ),
         name="out_scatter",
-    )(part, activations, b_down.reshape(1, -1))
-
-
-def rotate(values, positions):
-    half = ROT // 2
-    index = jnp.arange(half, dtype=jnp.float32)
-    freqs = jnp.power(jnp.float32(10000.0), -2.0 * index / ROT)
-    angle = positions[:, None, None] * freqs[None, None, :]
-    cosine = jnp.cos(angle)
-    sine = jnp.sin(angle)
-    pairs = values[..., :ROT].reshape(values.shape[:-1] + (half, 2))
-    first = pairs[..., 0]
-    second = pairs[..., 1]
-    turned = jnp.stack([first * cosine - second * sine, second * cosine + first * sine], axis=-1)
-    turned = turned.reshape(values.shape[:-1] + (ROT,))
-    return jnp.concatenate([turned, values[..., ROT:]], axis=-1)
+    )(part, att, w_out)
+
+
+def attention_kernel(own_count, lens, qkv, table, pk, pv, ok, ov, out):
+    rows = qkv.shape[1]
+    prompt = lens[pl.program_id(0)]
+    cosine, sine, own_len = table[0], table[1], table[2][:, 0:1]
+    even = lax.broadcasted_iota(jnp.int32, (rows, HS), 1) % 2 == 0
+
+    def turn(values):
+        swapped = jnp.where(
+            even, pltpu.roll(values, HS - 1, axis=1), pltpu.roll(values, 1, axis=1)
+        )
+        return (values * cosine + swapped * sine).astype(jnp.bfloat16)
+
+    query = turn(qkv[0])
+    key_new = turn(qkv[1])
+    value_new = qkv[2].astype(jnp.bfloat16).astype(jnp.float32)
+    scale = 1.0 / math.sqrt(HS)
+    contract = (((1,), (1,)), ((), ()))
+    mine_keys = ok[...].reshape(rows * own_count, HS)
+    mine_vals = ov[...].reshape(rows * own_count, HS)
+    pre = lax.dot_general(query, pk[0], contract, preferred_element_type=jnp.float32) * scale
+    own = lax.dot_general(query, mine_keys, contract, preferred_element_type=jnp.float32) * scale
+    me = (
+        jnp.sum(query.astype(jnp.float32) * key_new.astype(jnp.float32), axis=1, keepdims=True)
+        * scale
+    )
+    pre = jnp.where(lax.broadcasted_iota(jnp.int32, pre.shape, 1) < prompt, pre, -jnp.inf)
+    lane = lax.broadcasted_iota(jnp.int32, own.shape, 1)
+    row = lax.broadcasted_iota(jnp.int32, own.shape, 0)
+    token = lane - row * own_count
+    keep = jnp.logical_and(token >= 0, token.astype(jnp.float32) < own_len)
+    own = jnp.where(keep, own, -jnp.inf)
+    peak = jnp.maximum(
+        jnp.maximum(jnp.max(pre, axis=1, keepdims=True), jnp.max(own, axis=1, keepdims=True)), me
+    )
+    pre = jnp.exp(pre - peak)
+    own = jnp.exp(own - peak)
+    me = jnp.exp(me - peak)
+    denom = jnp.sum(pre, axis=1, keepdims=True) + jnp.sum(own, axis=1, keepdims=True) + me
+    mixed = jnp.dot(pre.astype(jnp.bfloat16), pv[0], preferred_element_type=jnp.float32)
+    mixed = mixed + jnp.dot(own.astype(jnp.bfloat16), mine_vals, preferred_element_type=jnp.float32)
+    mixed = mixed + me.astype(jnp.bfloat16).astype(jnp.float32) * value_new
+    out[...] = (mixed / denom).astype(jnp.bfloat16)
+
+
+def attention(qkv, prompt_len, own_len, pk, pv, ok, ov):
+    rows, width = qkv.shape[1], qkv.shape[2]
+    groups, longest = pk.shape[0], pk.shape[1]
+    own_count = ok.shape[1]
+    member = (jnp.arange(rows) // GSIZE)[:, None] == jnp.arange(groups)[None, :]
+    row_prompt = jnp.sum(jnp.where(member, prompt_len[None, :], 0), axis=1)
+    positions = (row_prompt + own_len).astype(jnp.float32)
+    lane = jnp.arange(HS)
+    index = (lane // 2).astype(jnp.float32)
+    freqs = jnp.where(lane < ROT, jnp.power(jnp.float32(10000.0), -2.0 * index / ROT), 0.0)
+    angle = positions[:, None] * freqs[None, :]
+    sign = jnp.where(lane % 2 == 0, -1.0, 1.0)
+    table = jnp.stack(
+        [
+            jnp.cos(angle),
+            jnp.sin(angle) * sign[None, :],
+            jnp.broadcast_to(own_len.astype(jnp.float32)[:, None], angle.shape),
+        ]
+    )
+    return pl.pallas_call(
+        functools.partial(attention_kernel, own_count),
+        out_shape=jax.ShapeDtypeStruct((rows, width), jnp.bfloat16),
+        grid=(groups, width // HS),
+        in_specs=[
+            pl.BlockSpec(memory_space=pltpu.SMEM),
+            pl.BlockSpec((3, GSIZE, HS), lambda i, j: (0, i, j)),
+            pl.BlockSpec((3, GSIZE, HS), lambda i, j: (0, i, 0)),
+            pl.BlockSpec((1, longest, HS), lambda i, j: (i, 0, j)),
+            pl.BlockSpec((1, longest, HS), lambda i, j: (i, 0, j)),
+            pl.BlockSpec((GSIZE, own_count, HS), lambda i, j: (i, 0, j)),
+            pl.BlockSpec((GSIZE, own_count, HS), lambda i, j: (i, 0, j)),
+        ],
+        out_specs=pl.BlockSpec((GSIZE, HS), lambda i, j: (i, j)),
+        compiler_params=pltpu.CompilerParams(vmem_limit_bytes=VMEM_LIMIT),
+        name="attention",
+    )(prompt_len, qkv, table, pk, pv, ok, ov)
 
 
 def local(
@@ -307,7 +406,6 @@
     head_count = lax.axis_size("head")
     width_here = activations.shape[1]
     local_rows = activations.shape[0]
-    groups_here = prompt_len.shape[0]
     gathered = gather_normed(activations, ln_gain, ln_bias)
     features = w_qkv.shape[0]
     columns = lax.dynamic_slice_in_dim(
@@ -319,64 +417,13 @@
         )
     )
     heads_here = w_qkv.shape[2] // HS
-    member = (jnp.arange(local_rows) // GSIZE)[:, None] == jnp.arange(groups_here)[None, :]
-    row_prompt = jnp.sum(jnp.where(member, prompt_len[None, :], 0), axis=1)
-    positions = (row_prompt + own_len).astype(jnp.float32)
-    query = rotate(qkv[0].reshape(local_rows, heads_here, HS), positions).astype(jnp.bfloat16)
-    key_new = rotate(qkv[1].reshape(local_rows, heads_here, HS), positions).astype(jnp.bfloat16)
-    value_new = qkv[2].reshape(local_rows, heads_here, HS).astype(jnp.bfloat16)
-    scale = 1.0 / math.sqrt(HS)
-    longest = prefix_keys.shape[1]
-    own_count = own_keys.shape[1]
-    grouped = query.reshape(groups_here, GSIZE, heads_here, HS)
-    pre_keys = prefix_keys.reshape(groups_here, longest, heads_here, HS)
-    pre_vals = prefix_values.reshape(groups_here, longest, heads_here, HS)
-    mine_keys = own_keys.reshape(local_rows, own_count, heads_here, HS)
-    mine_vals = own_values.reshape(local_rows, own_count, heads_here, HS)
-    pre_scores = (
-        jnp.einsum("gqhd,gjhd->gqhj", grouped, pre_keys, preferred_element_type=jnp.float32) * scale
-    )
-    pre_scores = jnp.where(
-        jnp.arange(longest)[None, None, None, :] < prompt_len[:, None, None, None],
-        pre_scores,
-        -jnp.inf,
-    )
-    own_scores = (
-        jnp.einsum("rhd,rthd->rht", query, mine_keys, preferred_element_type=jnp.float32) * scale
-    )
-    own_scores = jnp.where(
-        jnp.arange(own_count)[None, None, :] < own_len[:, None, None], own_scores, -jnp.inf
-    )
-    self_scores = (
-        jnp.einsum("rhd,rhd->rh", query, key_new, preferred_element_type=jnp.float32) * scale
-    )
-    pre_peak = jnp.max(pre_scores, axis=-1).reshape(local_rows, heads_here)
-    peak = jnp.maximum(jnp.maximum(pre_peak, jnp.max(own_scores, axis=-1)), self_scores)
-    pre_exp = jnp.exp(pre_scores - peak.reshape(groups_here, GSIZE, heads_here)[..., None])
-    own_exp = jnp.exp(own_scores - peak[..., None])
-    self_exp = jnp.exp(self_scores - peak)
-    denom = (
-        jnp.sum(pre_exp, axis=-1).reshape(local_rows, heads_here)
-        + jnp.sum(own_exp, axis=-1)
-        + self_exp
-    )
-    mixed = jnp.einsum(
-        "gqhj,gjhd->gqhd",
-        pre_exp.astype(jnp.bfloat16),
-        pre_vals,
-        preferred_element_type=jnp.float32,
-    )
-    mixed = mixed.reshape(local_rows, heads_here, HS)
-    mixed = mixed + jnp.einsum(
-        "rht,rthd->rhd", own_exp.astype(jnp.bfloat16), mine_vals, preferred_element_type=jnp.float32
-    )
-    mixed = mixed + self_exp.astype(jnp.bfloat16).astype(jnp.float32)[..., None] * value_new.astype(
-        jnp.float32
-    )
-    attended = (mixed / denom[..., None]).astype(jnp.bfloat16)
-    transposed = jnp.transpose(attended, (2, 1, 0))
-    slices = lax.all_to_all(transposed, "grp", split_axis=0, concat_axis=2, tiled=True)
-    dim_here = slices.shape[0]
+    attended = attention(
+        qkv, prompt_len, own_len, prefix_keys, prefix_values, own_keys, own_values
+    )
+    dim_here = w_attn_out.shape[0]
+    att = jnp.transpose(
+        attended.reshape(local_rows, heads_here, grp_count, dim_here), (2, 0, 3, 1)
+    ).reshape(grp_count, local_rows, dim_here * heads_here)
     hidden = jax.nn.gelu(
         jnp.dot(
             gathered,
@@ -386,15 +433,16 @@
         + b_in.astype(jnp.float32),
         approximate=True,
     ).astype(jnp.bfloat16)
-    attn_rows = jnp.transpose(
-        slices.reshape(dim_here * heads_here, grp_count * local_rows), (1, 0)
-    )
-    combined = jnp.dot(hidden, w_down, preferred_element_type=jnp.float32) + jnp.dot(
-        attn_rows,
+    mlp = jnp.dot(hidden, w_down, preferred_element_type=jnp.float32)
+    summed = out_scatter(
+        mlp,
+        att,
         w_attn_out.reshape(dim_here * heads_here, head_count * width_here),
-        preferred_element_type=jnp.float32,
-    )
-    return out_scatter(combined, activations, b_down)
+        local_rows,
+        width_here,
+    )
+    total = activations.astype(jnp.float32) + b_down.astype(jnp.float32)[None, :] + summed
+    return total.astype(jnp.bfloat16)
 
 
 def solution(mesh):

time: 145 us -> 125 us (0.86)
  Pallas kernels: 81.6 us -> 99.8 us
  matrix products: 28.2 us -> 11.6 us
  local copies, waits for them, and re-layouts: 16.3 us -> 7.67 us
  other arithmetic: 11.1 us -> 4.7 us
  starting transfers between devices: 3.99 us -> 0 us
  waiting for transfers between devices: 2.78 us -> 0 us
    dot_general x6 -> x1, matrix products: 25.1 us -> 8.54 us  [local(): mlp = jnp.dot(hidden, w_down, preferred_element_type=jnp.float32)]
    pallas_call x0 -> x1, Pallas kernels: none -> 10.4 us  [attention(): pl.pallas_call(functools.partial(attention_kernel, own_count), out_shape=...]
    pallas_call x1, Pallas kernels: 22.4 us -> 30.3 us  [out_scatter(): pl.pallas_call(functools.partial(out_kernel, zs), out_shape=jax.ShapeDtyp...]
    all_to_all x1 -> x0, starting transfers between devices: 3.99 us -> none  [local(): lax.all_to_all(transposed, 'grp', split_axis=0, concat_axis=2, tiled=True)]
    unnamed x16 -> x8, local copies, waits for them, and re-layouts: 3.63 us -> 0.02 us
    all_to_all x1 -> x0, waiting for transfers between devices: 2.78 us -> none  [local(): lax.all_to_all(transposed, 'grp', split_axis=0, concat_axis=2, tiled=True)]
    slice x5 -> x0, local copies, waits for them, and re-layouts: 2.48 us -> none  [the longest x2 1.46 us: rotate(): return jnp.concatenate([turned, values[..., ROT:]], axis=-1)]
    reshape x8 -> x3, local copies, waits for them, and re-layouts: 6.3 us -> 4.01 us  [the longest x2 2.28 us: local(): attended.reshape(local_rows, heads_here, grp_count, dim_here)]
  transfers between devices with their start and end apart: 1 -> 0, of which waited for: 1 -> 0; matrix products, arithmetic and copies ran while one was open for 3% -> 0% of each run, Pallas kernels for 0% -> 0%
where the time goes in v2:
time: 125 us; the launch traced here: 124 us
  Pallas kernels  99.8 us (80%)
  matrix products  11.6 us (9%)
  local copies, waits for them, and re-layouts  7.67 us (6%)
  other arithmetic  4.7 us (4%)
    pallas_call x1, Pallas kernels, gather_normed(): pl.pallas_call(functools.partial(gather_kernel, zs, heads), out_shape=jax...  31.1 us
    pallas_call x1, Pallas kernels, out_scatter(): pl.pallas_call(functools.partial(out_kernel, zs), out_shape=jax.ShapeDtyp...  30.3 us
    pallas_call x1, Pallas kernels, qkv_scatter(): pl.pallas_call(functools.partial(qkv_kernel, zs), out_shape=jax.ShapeDtyp...  28.1 us
    pallas_call x1, Pallas kernels, attention(): pl.pallas_call(functools.partial(attention_kernel, own_count), out_shape=...  10.4 us
    dot_general x1, matrix products, local(): mlp = jnp.dot(hidden, w_down, preferred_element_type=jnp.float32)  8.54 us
    dot_general x1, matrix products, local(): jnp.einsum('rf,fch->crh', columns, w_qkv, preferred_element_type=jnp.floa...  3.11 us

profile of v2, /device:TPU:0, one launch (start us, length us, event | category | flops | bytes accessed | tf_op | source)
XLA Modules:
  0.0 124.0 jit_solution(1509430919228329350)
XLA Ops:
  0.0 0.0 copy-start
  0.0 0.9 fusion.21
  0.9 0.7 add_convert_fusion.1
  1.6 0.2 multiply_cosine_fusion
  1.9 0.1 stack_broadcast_in_dim.2
  1.9 0.7 pad_maximum_fusion.table
  2.6 0.7 stack.14
  3.3 0.7 stack.15
  4.0 0.7 maximum_convert_fusion.affine
  4.7 31.1 %gather_normed.1 = bf16[256,4096]{1,0:T(8,128)(2,1)} custom-call(bf16[32,1024]{1,0:T(8,128)(2,1)} %act.1, f32[2,4096]{1,0:T(2,128)} %maximum_convert_fusion.affine), custom_call_target="tpu_custom_call" | custom-call | tf_op jit(solution)/shard_map/gather_normed/pallas_call | solution.py:119
  35.8 0.0 copy-done
  35.8 3.1 %fusion.part = bf16[3,256,1024]{2,1,0:T(8,128)(2,1)} fusion(bf16[512,3,1024]{2,0,1:T(8,128)(2,1)S(1)} %copy-done, bf16[256,4096]{1,0:T(8,128)(2,1)} %gather_normed.1, s32[]{:T(128)S(6)} %select_n.52), kind=kOutput, calls=%fused_computation.1 | convolution fusion | flops 806092800 | bytes 4980740 | tf_op jit(solution)/shard_map/rf,fch->crh/dot_general | solution.py:415
  38.9 28.1 %qkv_scatter.1.qkv = f32[3,32,1024]{2,1,0:T(8,128)} custom-call(bf16[3,256,1024]{2,1,0:T(8,128)(2,1)} %fusion.part), custom_call_target="tpu_custom_call" | custom-call | tf_op jit(solution)/shard_map/qkv_scatter/pallas_call | solution.py:173
  67.0 0.0 copy-start.3
  67.0 10.4 %attention.1 = bf16[32,1024]{1,0:T(8,128)(2,1)} custom-call(s32[2]{0:T(128)} %lens.1, f32[3,32,1024]{2,1,0:T(8,128)} %qkv_scatter.1.qkv, f32[3,32,256]{2,1,0:T(8,128)} %pad_maximum_fusion.table, bf16[2,1024,1024]{2,1,0:T(8,128)(2,1)} %pk.1, bf16[2,1024,1024]{2,1,0:T(8,128)(2,1)} %pv.1, bf16[32,32,1024]{2,1,0:T(8,128)(2,1)} %ok.1, bf16[32,32,1024]{2,1,0:T(8,128)(2,1)} %ov.1), custom_call_target="tpu_custom_call" | custom-call | tf_op jit(solution)/shard_map/attention/pallas_call | solution.py:369
  77.4 1.1 reshape.164
  78.5 1.2 copy.19
  79.7 1.7 %copy.20.att = bf16[8,32,128]{2,1,0:T(8,128)(2,1)} copy(bf16[8,32,128]{1,0,2:T(8,128)(2,1)} %bitcast.12) | data formatting | bytes 131072 | tf_op jit(solution)/shard_map/reshape | solution.py:426
  81.4 0.0 copy-done.3
  81.4 8.5 %fusion.9.part = f32[256,4096]{1,0:T(8,128)} fusion(bf16[512,4096]{1,0:T(8,128)(2,1)} %param.28, bf16[256,4096]{1,0:T(8,128)(2,1)} %gather_normed.1, bf16[4096,512]{1,0:T(8,128)(2,1)} %param.26, f32[512]{0:T(512)S(1)} %convert_element_type.39), kind=kOutput, calls=%fused_computation.12 | convolution fusion | flops 2148794368 | bytes 14682112 | tf_op jit(solution)/shard_map/dot_general | solution.py:436
  90.0 2.1 %reshape.166.w_out = bf16[128,4096]{1,0:T(8,128)(2,1)} reshape(bf16[32,4,4096]{2,1,0:T(4,128)(2,1)} %param.25) | data formatting | bytes 2097152 | tf_op jit(solution)/shard_map/reshape | solution.py:440
  92.1 30.3 %out_scatter.1 = f32[32,1024]{1,0:T(8,128)} custom-call(f32[256,4096]{1,0:T(8,128)} %fusion.9.part, bf16[8,32,128]{2,1,0:T(8,128)(2,1)} %copy.20.att, bf16[128,4096]{1,0:T(8,128)(2,1)} %reshape.166.w_out), custom_call_target="tpu_custom_call" | custom-call | tf_op jit(solution)/shard_map/out_scatter/pallas_call | solution.py:283
  122.4 0.0 copy-done.1
  122.4 1.6 %add_convert_fusion = bf16[32,1024]{1,0:T(8,128)(2,1)} fusion(f32[32,1024]{1,0:T(8,128)} %out_scatter.1, bf16[32,1024]{1,0:T(8,128)(2,1)S(1)} %copy-done.1, f32[1024]{0:T(1024)S(1)} %convert_element_type.37), kind=kLoop, calls=%fused_computation.20 | loop fusion | flops 131072 | bytes 266240 | tf_op jit(solution)/shard_map/convert_element_type | solution.py:445
  (7 shorter events, 0.0 us)
Async XLA Ops:
  0.0 35.8 %copy-start = (bf16[512,3,1024]{2,0,1:T(8,128)(2,1)S(1)}, bf16[512,3,1024]{2,0,1:T(8,128)(2,1)}, u32[]{:S(2)}) copy-start(bf16[512,3,1024]{2,0,1:T(8,128)(2,1)} %param.18) | copy-start | bytes 9437188
  67.0 14.4 %copy-start.3 = (bf16[512]{0:T(512)(128)(2,1)S(1)}, bf16[512]{0:T(512)(128)(2,1)}, u32[]{:S(2)}) copy-start(bf16[512]{0:T(512)(128)(2,1)} %param.27) | copy-start | bytes 3076
  92.1 30.3 %copy-start.2 = (bf16[1024]{0:T(1024)(128)(2,1)S(1)}, bf16[1024]{0:T(1024)(128)(2,1)}, u32[]{:S(2)}) copy-start(bf16[1024]{0:T(1024)(128)(2,1)} %param.29) | copy-start | bytes 6148
  92.1 30.3 %copy-start.1 = (bf16[32,1024]{1,0:T(8,128)(2,1)S(1)}, bf16[32,1024]{1,0:T(8,128)(2,1)}, u32[]{:S(2)}) copy-start(bf16[32,1024]{1,0:T(8,128)(2,1)} %act.1) | copy-start | bytes 196612

commit v3 on v2

--- a/solution.py
+++ b/solution.py
@@ -129,7 +129,13 @@
     )(activations, jnp.stack([gain, shift]).astype(jnp.float32))
 
 
-def qkv_kernel(zs, part, out, r3, s4, r4, ys, yr, zsend, zr):
+def qkv_kernel(
+    zs, part, normed, w_in, b_in, w_down, out, mlp, wi, wd, hid, held, r3, s4, r4, ys, yr, zsend, zr
+):
+    load_in = pltpu.make_async_copy(w_in, wi, held.at[0])
+    load_in.start()
+    load_down = pltpu.make_async_copy(w_down, wd, held.at[1])
+    load_down.start()
     g, h, z, y, x, c = place(zs)
     rows = out.shape[1]
     yg = z * 2 + (1 - y)
@@ -145,6 +151,34 @@
     for k in turns:
         ycopies[k] = remote(part.at[:, block(k, 1 - y), :], r3.at[k], ys.at[k], yr.at[k], (yg, h))
         ycopies[k].start()
+    high = 256
+    wide = min(256, wi.shape[1])
+    across = wi.shape[1] // wide
+    load_in.wait()
+
+    @pl.loop(0, (normed.shape[0] // high) * across)
+    def _(t):
+        band = pl.ds(pl.multiple_of((t // across) * high, high), high)
+        columns = pl.ds(pl.multiple_of((t % across) * wide, wide), wide)
+        value = jnp.dot(normed[band, :], wi[:, columns], preferred_element_type=jnp.float32)
+        value = value + b_in[:, columns]
+        inner = math.sqrt(2.0 / math.pi) * (value + 0.044715 * (value * value * value))
+        hid[band, columns] = (0.5 * value * (1.0 + jnp.tanh(inner))).astype(jnp.bfloat16)
+
+    tile = 512
+    tiles = wd.shape[1] // tile
+    steps = (normed.shape[0] // high) * tiles
+    load_down.wait()
+
+    def down(first, last):
+        @pl.loop(first, last)
+        def _(t):
+            band = pl.ds(pl.multiple_of((t // tiles) * high, high), high)
+            columns = pl.ds(pl.multiple_of((t % tiles) * tile, tile), tile)
+            mlp[band, columns] = jnp.dot(
+                hid[band, :], wd[:, columns], preferred_element_type=jnp.float32
+            ).astype(mlp.dtype)
+
     zcopies = []
     for k in range(1, zs):
         ycopies[k].wait_recv()
@@ -153,6 +187,7 @@
         copy = remote(s4.at[k], r4.at[k], zsend.at[k], zr.at[k], zpeers[k - 1])
         copy.start()
         zcopies.append(copy)
+        down(steps * (k - 1) // (zs - 1), steps * k // (zs - 1))
     ycopies[0].wait_recv()
     total = part[:, block(0, y), :].astype(jnp.float32) + r3[0].astype(jnp.float32)
     for k in range(1, zs):
@@ -165,22 +200,38 @@
         copy.wait_send()
 
 
-def qkv_scatter(part):
+def qkv_scatter(part, normed, w_in, b_in, w_down):
     groups = lax.axis_size("grp")
     zs = groups // 2
     rows, width = part.shape[1] // groups, part.shape[2]
     buffer = pltpu.VMEM((zs, 3, rows, width), jnp.bfloat16)
     return pl.pallas_call(
         functools.partial(qkv_kernel, zs),
-        out_shape=jax.ShapeDtypeStruct((3, rows, width), jnp.float32),
-        in_specs=[VMEM_SPEC],
-        out_specs=VMEM_SPEC,
-        scratch_shapes=[buffer] * 3 + [DMA((zs,))] * 4,
+        out_shape=(
+            jax.ShapeDtypeStruct((3, rows, width), jnp.float32),
+            jax.ShapeDtypeStruct((part.shape[1], w_down.shape[1]), jnp.bfloat16),
+        ),
+        in_specs=[
+            VMEM_SPEC,
+            VMEM_SPEC,
+            pl.BlockSpec(memory_space=pl.ANY),
+            VMEM_SPEC,
+            pl.BlockSpec(memory_space=pl.ANY),
+        ],
+        out_specs=(VMEM_SPEC, VMEM_SPEC),
+        scratch_shapes=[
+            pltpu.VMEM(w_in.shape, jnp.bfloat16),
+            pltpu.VMEM(w_down.shape, jnp.bfloat16),
+            pltpu.VMEM((part.shape[1], w_in.shape[1]), jnp.bfloat16),
+            DMA((2,)),
+        ]
+        + [buffer] * 3
+        + [DMA((zs,))] * 4,
         compiler_params=pltpu.CompilerParams(
             collective_id=1, has_side_effects=True, vmem_limit_bytes=VMEM_LIMIT
         ),
         name="qkv_scatter",
-    )(part)
+    )(part, normed, w_in, b_in.astype(jnp.float32).reshape(1, -1), w_down)
 
 
 def out_kernel(zs, part, att, w_out, out, acc, ra, asend, arecv, s1, r1, s2, r2, s3, r3, s4, r4, cs, cr, xs, xr, ys, yr, zsend, zr):
@@ -214,7 +265,7 @@
     @pl.loop(0, part.shape[1] // tile)
     def _(t):
         columns = pl.ds(pl.multiple_of(t * tile, tile), tile)
-        acc[:, columns] = part[:, columns] + jnp.dot(
+        acc[:, columns] = part[:, columns].astype(jnp.float32) + jnp.dot(
             ra[...], w_out[:, columns], preferred_element_type=jnp.float32
         )
 
@@ -411,10 +462,14 @@
     columns = lax.dynamic_slice_in_dim(
         gathered, lax.axis_index("grp") * features, features, axis=1
     )
-    qkv = qkv_scatter(
+    qkv, mlp = qkv_scatter(
         jnp.einsum("rf,fch->crh", columns, w_qkv, preferred_element_type=jnp.float32).astype(
             jnp.bfloat16
-        )
+        ),
+        gathered,
+        w_in,
+        b_in,
+        w_down,
     )
     heads_here = w_qkv.shape[2] // HS
     attended = attention(
@@ -424,16 +479,6 @@
     att = jnp.transpose(
         attended.reshape(local_rows, heads_here, grp_count, dim_here), (2, 0, 3, 1)
     ).reshape(grp_count, local_rows, dim_here * heads_here)
-    hidden = jax.nn.gelu(
-        jnp.dot(
-            gathered,
-            w_in,
-            preferred_element_type=jnp.float32,
-        )
-        + b_in.astype(jnp.float32),
-        approximate=True,
-    ).astype(jnp.bfloat16)
-    mlp = jnp.dot(hidden, w_down, preferred_element_type=jnp.float32)
     summed = out_scatter(
         mlp,
         att,

time: 125 us -> 116 us (0.928)
  matrix products: 11.6 us -> 3.12 us
    dot_general x1 -> x0, matrix products: 8.54 us -> none  [local(): mlp = jnp.dot(hidden, w_down, preferred_element_type=jnp.float32)]
    pallas_call x1, Pallas kernels: 28.1 us -> 29.5 us  [qkv_scatter(): pl.pallas_call(functools.partial(qkv_kernel, zs), out_shape=(jax.ShapeDty...]
where the time goes in v3:
time: 116 us; the launch traced here: 115 us
  Pallas kernels  101 us (87%)
  local copies, waits for them, and re-layouts  7.93 us (7%)
  other arithmetic  3.74 us (3%)
  matrix products  3.12 us (3%)
    pallas_call x1, Pallas kernels, gather_normed(): pl.pallas_call(functools.partial(gather_kernel, zs, heads), out_shape=jax...  31.1 us
    pallas_call x1, Pallas kernels, out_scatter(): pl.pallas_call(functools.partial(out_kernel, zs), out_shape=jax.ShapeDtyp...  29.6 us
    pallas_call x1, Pallas kernels, qkv_scatter(): pl.pallas_call(functools.partial(qkv_kernel, zs), out_shape=(jax.ShapeDty...  29.5 us
    pallas_call x1, Pallas kernels, attention(): pl.pallas_call(functools.partial(attention_kernel, own_count), out_shape=...  10.3 us
    dot_general x1, matrix products, local(): jnp.einsum('rf,fch->crh', columns, w_qkv, preferred_element_type=jnp.floa...  3.12 us

profile of v3, /device:TPU:0, one launch (start us, length us, event | category | flops | bytes accessed | tf_op | source)
XLA Modules:
  0.0 115.4 jit_solution(6670304330670675045)
XLA Ops:
  0.0 0.0 copy-start
  0.0 0.9 stack.14
  0.9 0.8 stack.15
  1.7 0.7 maximum_convert_fusion.affine
  2.3 31.1 %gather_normed.1.normed = bf16[256,4096]{1,0:T(8,128)(2,1)} custom-call(bf16[32,1024]{1,0:T(8,128)(2,1)} %act.1, f32[2,4096]{1,0:T(2,128)} %maximum_convert_fusion.affine), custom_call_target="tpu_custom_call" | custom-call | tf_op jit(solution)/shard_map/gather_normed/pallas_call | solution.py:119
  33.5 3.1 %fusion.part = bf16[3,256,1024]{2,1,0:T(8,128)(2,1)} fusion(bf16[512,3,1024]{2,0,1:T(8,128)(2,1)S(1)} %copy-done, bf16[256,4096]{1,0:T(8,128)(2,1)} %gather_normed.1.normed, s32[]{:T(128)S(6)} %select_n.52), kind=kOutput, calls=%fused_computation.1 | convolution fusion | flops 806092800 | bytes 4980740 | tf_op jit(solution)/shard_map/rf,fch->crh/dot_general | solution.py:466
  36.6 0.0 copy-done.3
  36.6 0.6 reshape.173
  37.2 29.5 %qkv_scatter.1 = (f32[3,32,1024]{2,1,0:T(8,128)}, bf16[256,4096]{1,0:T(8,128)(2,1)}) custom-call(bf16[3,256,1024]{2,1,0:T(8,128)(2,1)} %fusion.part, bf16[256,4096]{1,0:T(8,128)(2,1)} %gather_normed.1.normed, bf16[4096,512]{1,0:T(8,128)(2,1)} %w_in.1, f32[1,512]{1,0:T(1,128)} %bitcast.11, bf16[512,4096]{1,0:T(8,128)(2,1)} %w_down.1), custom_call_target="tpu_custom_call" | custom-call | tf_op jit(solution)/shard_map/qkv_scatter/pallas_call | solution.py:208
  66.7 0.0 copy-done.4
  66.7 0.1 fusion.7
  66.8 0.2 multiply_cosine_fusion
  67.0 0.1 stack_broadcast_in_dim.2
  67.1 0.6 pad_maximum_fusion.table
  67.7 10.3 %attention.1 = bf16[32,1024]{1,0:T(8,128)(2,1)} custom-call(s32[2]{0:T(128)} %lens.1, f32[3,32,1024]{2,1,0:T(8,128)} %get-tuple-element.8.qkv, f32[3,32,256]{2,1,0:T(8,128)} %pad_maximum_fusion.table, bf16[2,1024,1024]{2,1,0:T(8,128)(2,1)} %pk.1, bf16[2,1024,1024]{2,1,0:T(8,128)(2,1)} %pv.1, bf16[32,32,1024]{2,1,0:T(8,128)(2,1)} %ok.1, bf16[32,32,1024]{2,1,0:T(8,128)(2,1)} %ov.1), custom_call_target="tpu_custom_call" | custom-call | tf_op jit(solution)/shard_map/attention/pallas_call | solution.py:420
  78.1 1.1 reshape.170
  79.1 0.0 copy-start.2
  79.1 0.0 copy-start.1
  79.2 1.2 %copy.19 = bf16[32,4,8,32]{0,2,1,3:T(8,128)(2,1)} copy(bf16[32,4,8,32]{3,2,1,0:T(8,128)(2,1)S(1)} %reshape.170) | data formatting | bytes 131072 | tf_op jit(solution)/shard_map/reshape | solution.py:480
  80.4 1.7 %copy.20.att = bf16[8,32,128]{2,1,0:T(8,128)(2,1)} copy(bf16[8,32,128]{1,0,2:T(8,128)(2,1)} %bitcast.10) | data formatting | bytes 131072 | tf_op jit(solution)/shard_map/reshape | solution.py:481
  82.1 2.2 %reshape.172.w_out = bf16[128,4096]{1,0:T(8,128)(2,1)} reshape(bf16[32,4,4096]{2,1,0:T(4,128)(2,1)} %param.25) | data formatting | bytes 2097152 | tf_op jit(solution)/shard_map/reshape | solution.py:485
  84.3 29.6 %out_scatter.1 = f32[32,1024]{1,0:T(8,128)} custom-call(bf16[256,4096]{1,0:T(8,128)(2,1)} %get-tuple-element.7.part, bf16[8,32,128]{2,1,0:T(8,128)(2,1)} %copy.20.att, bf16[128,4096]{1,0:T(8,128)(2,1)} %reshape.172.w_out), custom_call_target="tpu_custom_call" | custom-call | tf_op jit(solution)/shard_map/out_scatter/pallas_call | solution.py:334
  113.9 0.0 copy-done.1
  113.9 1.6 %add_convert_fusion = bf16[32,1024]{1,0:T(8,128)(2,1)} fusion(f32[32,1024]{1,0:T(8,128)} %out_scatter.1, bf16[32,1024]{1,0:T(8,128)(2,1)S(1)} %copy-done.1, f32[1024]{0:T(1024)S(1)} %convert_element_type.32), kind=kLoop, calls=%fused_computation.4 | loop fusion | flops 131072 | bytes 266240 | tf_op jit(solution)/shard_map/convert_element_type | solution.py:490
  (10 shorter events, 0.0 us)
Async XLA Ops:
  0.0 33.4 %copy-start = (bf16[512,3,1024]{2,0,1:T(8,128)(2,1)S(1)}, bf16[512,3,1024]{2,0,1:T(8,128)(2,1)}, u32[]{:S(2)}) copy-start(bf16[512,3,1024]{2,0,1:T(8,128)(2,1)} %param.18) | copy-start | bytes 9437188
  2.3 34.2 %copy-start.3 = (bf16[512]{0:T(512)(128)(2,1)S(1)}, bf16[512]{0:T(512)(128)(2,1)}, u32[]{:S(2)}) copy-start(bf16[512]{0:T(512)(128)(2,1)} %param.27) | copy-start | bytes 3076
  37.2 29.5 %copy-start.4 = (s32[2]{0:T(128)S(1)}, s32[2]{0:T(128)}, u32[]{:S(2)}) copy-start(s32[2]{0:T(128)} %lens.1) | copy-start | bytes 28
  37.2 29.6 %copy-start.5 = (s32[32]{0:T(128)S(1)}, s32[32]{0:T(128)}, u32[]{:S(2)}) copy-start(s32[32]{0:T(128)} %param.24) | copy-start | bytes 388
  79.1 34.7 %copy-start.2 = (bf16[1024]{0:T(1024)(128)(2,1)S(1)}, bf16[1024]{0:T(1024)(128)(2,1)}, u32[]{:S(2)}) copy-start(bf16[1024]{0:T(1024)(128)(2,1)} %param.29) | copy-start | bytes 6148
  79.1 34.7 %copy-start.1 = (bf16[32,1024]{1,0:T(8,128)(2,1)S(1)}, bf16[32,1024]{1,0:T(8,128)(2,1)}, u32[]{:S(2)}) copy-start(bf16[32,1024]{1,0:T(8,128)(2,1)} %act.1) | copy-start | bytes 196612

commit v4 on v3

--- a/solution.py
+++ b/solution.py
@@ -126,7 +126,7 @@
             collective_id=0, has_side_effects=True, vmem_limit_bytes=VMEM_LIMIT
         ),
         name="gather_normed",
-    )(activations, jnp.stack([gain, shift]).astype(jnp.float32))
+    )(activations, jnp.stack([gain.astype(jnp.float32), shift.astype(jnp.float32)]))
 
 
 def qkv_kernel(

time: 116 us -> 116 us (level)
  no operation moved by 1% of the time
where the time goes in v4:
time: 116 us; the launch traced here: 115 us
  Pallas kernels  101 us (87%)
  local copies, waits for them, and re-layouts  7.93 us (7%)
  other arithmetic  3.74 us (3%)
  matrix products  3.12 us (3%)
    pallas_call x1, Pallas kernels, gather_normed(): pl.pallas_call(functools.partial(gather_kernel, zs, heads), out_shape=jax...  31.1 us
    pallas_call x1, Pallas kernels, out_scatter(): pl.pallas_call(functools.partial(out_kernel, zs), out_shape=jax.ShapeDtyp...  29.6 us
    pallas_call x1, Pallas kernels, qkv_scatter(): pl.pallas_call(functools.partial(qkv_kernel, zs), out_shape=(jax.ShapeDty...  29.5 us
    pallas_call x1, Pallas kernels, attention(): pl.pallas_call(functools.partial(attention_kernel, own_count), out_shape=...  10.3 us
    dot_general x1, matrix products, local(): jnp.einsum('rf,fch->crh', columns, w_qkv, preferred_element_type=jnp.floa...  3.12 us

profile of v4, /device:TPU:0, one launch (start us, length us, event | category | flops | bytes accessed | tf_op | source)
XLA Modules:
  0.0 115.4 jit_solution(6670304330670675045)
XLA Ops:
  0.0 0.0 copy-start
  0.0 0.9 stack.18
  0.9 0.8 stack.19
  1.7 0.7 maximum_convert_fusion.affine
  2.3 31.1 %gather_normed.1.normed = bf16[256,4096]{1,0:T(8,128)(2,1)} custom-call(bf16[32,1024]{1,0:T(8,128)(2,1)} %act.1, f32[2,4096]{1,0:T(2,128)} %maximum_convert_fusion.affine), custom_call_target="tpu_custom_call" | custom-call | tf_op jit(solution)/shard_map/gather_normed/pallas_call | solution.py:119
  33.5 3.1 %fusion.part = bf16[3,256,1024]{2,1,0:T(8,128)(2,1)} fusion(bf16[512,3,1024]{2,0,1:T(8,128)(2,1)S(1)} %copy-done, bf16[256,4096]{1,0:T(8,128)(2,1)} %gather_normed.1.normed, s32[]{:T(128)S(6)} %select_n.52), kind=kOutput, calls=%fused_computation.1 | convolution fusion | flops 806092800 | bytes 4980740 | tf_op jit(solution)/shard_map/rf,fch->crh/dot_general | solution.py:466
  36.6 0.0 copy-done.3
  36.6 0.6 reshape.173
  37.2 29.5 %qkv_scatter.1 = (f32[3,32,1024]{2,1,0:T(8,128)}, bf16[256,4096]{1,0:T(8,128)(2,1)}) custom-call(bf16[3,256,1024]{2,1,0:T(8,128)(2,1)} %fusion.part, bf16[256,4096]{1,0:T(8,128)(2,1)} %gather_normed.1.normed, bf16[4096,512]{1,0:T(8,128)(2,1)} %w_in.1, f32[1,512]{1,0:T(1,128)} %bitcast.11, bf16[512,4096]{1,0:T(8,128)(2,1)} %w_down.1), custom_call_target="tpu_custom_call" | custom-call | tf_op jit(solution)/shard_map/qkv_scatter/pallas_call | solution.py:208
  66.7 0.0 copy-done.4
  66.7 0.1 fusion.7
  66.8 0.2 multiply_cosine_fusion
  67.0 0.1 stack_broadcast_in_dim.2
  67.1 0.6 pad_maximum_fusion.table
  67.7 10.3 %attention.1 = bf16[32,1024]{1,0:T(8,128)(2,1)} custom-call(s32[2]{0:T(128)} %lens.1, f32[3,32,1024]{2,1,0:T(8,128)} %get-tuple-element.8.qkv, f32[3,32,256]{2,1,0:T(8,128)} %pad_maximum_fusion.table, bf16[2,1024,1024]{2,1,0:T(8,128)(2,1)} %pk.1, bf16[2,1024,1024]{2,1,0:T(8,128)(2,1)} %pv.1, bf16[32,32,1024]{2,1,0:T(8,128)(2,1)} %ok.1, bf16[32,32,1024]{2,1,0:T(8,128)(2,1)} %ov.1), custom_call_target="tpu_custom_call" | custom-call | tf_op jit(solution)/shard_map/attention/pallas_call | solution.py:420
  78.1 1.1 reshape.170
  79.1 0.0 copy-start.2
  79.1 0.0 copy-start.1
  79.2 1.2 %copy.19 = bf16[32,4,8,32]{0,2,1,3:T(8,128)(2,1)} copy(bf16[32,4,8,32]{3,2,1,0:T(8,128)(2,1)S(1)} %reshape.170) | data formatting | bytes 131072 | tf_op jit(solution)/shard_map/reshape | solution.py:480
  80.4 1.7 %copy.20.att = bf16[8,32,128]{2,1,0:T(8,128)(2,1)} copy(bf16[8,32,128]{1,0,2:T(8,128)(2,1)} %bitcast.10) | data formatting | bytes 131072 | tf_op jit(solution)/shard_map/reshape | solution.py:481
  82.1 2.2 %reshape.172.w_out = bf16[128,4096]{1,0:T(8,128)(2,1)} reshape(bf16[32,4,4096]{2,1,0:T(4,128)(2,1)} %param.25) | data formatting | bytes 2097152 | tf_op jit(solution)/shard_map/reshape | solution.py:485
  84.3 29.6 %out_scatter.1 = f32[32,1024]{1,0:T(8,128)} custom-call(bf16[256,4096]{1,0:T(8,128)(2,1)} %get-tuple-element.7.part, bf16[8,32,128]{2,1,0:T(8,128)(2,1)} %copy.20.att, bf16[128,4096]{1,0:T(8,128)(2,1)} %reshape.172.w_out), custom_call_target="tpu_custom_call" | custom-call | tf_op jit(solution)/shard_map/out_scatter/pallas_call | solution.py:334
  113.9 0.0 copy-done.1
  113.9 1.6 %add_convert_fusion = bf16[32,1024]{1,0:T(8,128)(2,1)} fusion(f32[32,1024]{1,0:T(8,128)} %out_scatter.1, bf16[32,1024]{1,0:T(8,128)(2,1)S(1)} %copy-done.1, f32[1024]{0:T(1024)S(1)} %convert_element_type.31), kind=kLoop, calls=%fused_computation.4 | loop fusion | flops 131072 | bytes 266240 | tf_op jit(solution)/shard_map/convert_element_type | solution.py:490
  (10 shorter events, 0.0 us)
Async XLA Ops:
  0.0 33.4 %copy-start = (bf16[512,3,1024]{2,0,1:T(8,128)(2,1)S(1)}, bf16[512,3,1024]{2,0,1:T(8,128)(2,1)}, u32[]{:S(2)}) copy-start(bf16[512,3,1024]{2,0,1:T(8,128)(2,1)} %param.18) | copy-start | bytes 9437188
  2.3 34.2 %copy-start.3 = (bf16[512]{0:T(512)(128)(2,1)S(1)}, bf16[512]{0:T(512)(128)(2,1)}, u32[]{:S(2)}) copy-start(bf16[512]{0:T(512)(128)(2,1)} %param.27) | copy-start | bytes 3076
  37.2 29.5 %copy-start.4 = (s32[2]{0:T(128)S(1)}, s32[2]{0:T(128)}, u32[]{:S(2)}) copy-start(s32[2]{0:T(128)} %lens.1) | copy-start | bytes 28
  37.2 29.6 %copy-start.5 = (s32[32]{0:T(128)S(1)}, s32[32]{0:T(128)}, u32[]{:S(2)}) copy-start(s32[32]{0:T(128)} %param.24) | copy-start | bytes 388
  79.1 34.7 %copy-start.2 = (bf16[1024]{0:T(1024)(128)(2,1)S(1)}, bf16[1024]{0:T(1024)(128)(2,1)}, u32[]{:S(2)}) copy-start(bf16[1024]{0:T(1024)(128)(2,1)} %param.29) | copy-start | bytes 6148
  79.1 34.7 %copy-start.1 = (bf16[32,1024]{1,0:T(8,128)(2,1)S(1)}, bf16[32,1024]{1,0:T(8,128)(2,1)}, u32[]{:S(2)}) copy-start(bf16[32,1024]{1,0:T(8,128)(2,1)} %act.1) | copy-start | bytes 196612
